TPU v7x, 256 devices: a whole 4x4x8 slice. The times are simulated.
256 devices in a mesh: ctx: 32 (over z_hi, y, x), exp: 8 (over z_lo, core).
Axes of the slice: x: 4, y: 4, z: 8 (z_hi: 2, z_lo: 4; z = z_hi * 4 + z_lo), core: 2. Of those that a mesh axis runs over, the one named last changes fastest.
Arguments:
- queries: bfloat16 [4096, 5120], P('ctx', 'exp'), may hold values from -4.6 to 4.6
- keys: bfloat16 [4096, 1024], P('ctx', 'exp'), may hold values from -4.6 to 4.6
- values: bfloat16 [4096, 1024], P('ctx', 'exp'), may hold values from -6 to 6
- block_order: int32 [64], replicated, may hold values from 0 to 63, each once
- routes: int32 [4096, 1], P('ctx'), may hold values from 0 to 7; in each aligned block of 128 rows (0 to 127, 128 to 255, ...) at most 32 rows name the same one
- norm_gain: float32 [5120], replicated, may hold values from 0.1 to 1.9
- router: float32 [5120, 8], replicated, may hold values from -0.078125 to 0.078125
- w_gate: bfloat16 [8, 5120, 8192], P('exp', None, 'ctx'), may hold values from -0.078125 to 0.078125
- w_up: bfloat16 [8, 5120, 8192], P('exp', None, 'ctx'), may hold values from -0.078125 to 0.078125
- w_down: bfloat16 [8, 8192, 5120], P('exp', 'ctx'), may hold values from -0.0625 to 0.0625
Outputs:
- attended: bfloat16 [4096, 5120], P('ctx', 'exp')
- routed: bfloat16 [4096, 5120], P('ctx', 'exp')
Inputs may be any that keep to these rules, and one draw needn't show every extreme that they name: `routes`: in the rows of one index of ctx (aligned blocks of 128 rows) no expert is named more than 32 times. `block_order`: A permutation of 0 to 63.
All inputs are finite; a program needn't handle non-finite values.
Results may differ from a plain program's by a relative error of at most 0.03.
Values may be sent and summed in bfloat16 or wider, within the bound.
A program may use at most 128 MiB of HBM per device.

v0:
```python
import math

import jax
import jax.numpy as jnp
from jax import lax
from jax.sharding import PartitionSpec as P

HEAD_DIM = 128
CAP = 32


def per_device(queries, keys, values, block_order, routes, norm_gain, router, w_gate, w_up, w_down):
    rows_here = queries.shape[0]
    ctx_count = lax.axis_size("ctx")
    exp_count = lax.axis_size("exp")
    ctx_index = lax.axis_index("ctx")
    exp_index = lax.axis_index("exp")
    kv_local = keys.shape[1] // HEAD_DIM
    q_local = queries.shape[1] // HEAD_DIM
    per_group = q_local // kv_local
    half_rows = rows_here // 2
    everywhere = jnp.arange(rows_here * ctx_count, dtype=jnp.int32)
    position = block_order[everywhere // half_rows] * half_rows + everywhere % half_rows
    query_pos = lax.dynamic_slice_in_dim(position, ctx_index * rows_here, rows_here)
    grouped = queries.reshape(rows_here, kv_local, per_group, HEAD_DIM)
    score_scale = 1.0 / math.sqrt(HEAD_DIM)
    running_max = jnp.full((kv_local, per_group, rows_here), -1e30, jnp.float32)
    key_piece = lax.all_gather(keys, "ctx", axis=0, tiled=True)
    value_piece = lax.all_gather(values, "ctx", axis=0, tiled=True)
    piece_rows = key_piece.shape[0]
    scores = (
        jnp.einsum(
            "sgqd,rgd->gqsr",
            grouped,
            key_piece.reshape(piece_rows, kv_local, HEAD_DIM),
            preferred_element_type=jnp.float32,
        )
        * score_scale
    )
    allowed = position[None, :] <= query_pos[:, None]
    scores = jnp.where(allowed, scores, -1e30)
    newest_max = jnp.maximum(running_max, jnp.max(scores, axis=3))
    weights = jnp.where(allowed, jnp.exp(scores - newest_max[..., None]), 0.0)
    running_sum = jnp.sum(weights, axis=3)
    weighted = jnp.einsum(
        "gqsr,rgd->gqsd",
        weights.astype(jnp.bfloat16),
        value_piece.reshape(piece_rows, kv_local, HEAD_DIM),
        preferred_element_type=jnp.float32,
    )
    running_max, running_sum, weighted = (newest_max, running_sum, weighted)
    attended = (
        (weighted / running_sum[..., None])
        .transpose(2, 0, 1, 3)
        .reshape(rows_here, q_local * HEAD_DIM)
    )
    attended = attended.astype(jnp.bfloat16)
    experts = router.shape[1]
    local_experts = w_gate.shape[0]
    capacity = CAP
    features = attended.shape[1]
    width = features * exp_count
    expert_id = routes[:, 0]
    onehot = (expert_id[:, None] == jnp.arange(experts, dtype=jnp.int32)[None, :]).astype(jnp.int32)
    earlier_count = jnp.cumsum(onehot, axis=0) - onehot
    slot_index = jnp.sum(earlier_count * onehot, axis=1)
    slot_code = slot_index * experts + expert_id
    placing = (
        jnp.arange(capacity * experts, dtype=jnp.int32)[:, None] == slot_code[None, :]
    ).astype(jnp.bfloat16)
    values_f32 = attended.astype(jnp.float32)
    gain_here = lax.dynamic_slice_in_dim(norm_gain, exp_index * features, features)
    scaled = values_f32 * gain_here[None, :]
    router_here = lax.dynamic_slice_in_dim(router, exp_index * features, features, 0)
    squares, partial_value = lax.psum(
        (
            jnp.sum(values_f32 * values_f32, axis=1),
            jnp.dot(scaled, router_here, precision=lax.Precision.HIGHEST),
        ),
        "exp",
    )
    inverse = lax.rsqrt(squares / width + 1e-05)
    logits = partial_value * inverse[:, None]
    gate_value = jax.nn.sigmoid(jnp.sum(jnp.where(onehot > 0, logits, 0.0), axis=1))
    outgoing = (scaled * (inverse * gate_value)[:, None]).astype(jnp.bfloat16)
    outbound = jnp.dot(placing, outgoing, preferred_element_type=jnp.float32).astype(jnp.bfloat16)
    outbound = outbound.reshape(capacity, experts, features)
    arrived = lax.all_to_all(outbound, "exp", split_axis=1, concat_axis=2, tiled=True)
    portion = lax.all_gather(arrived, "ctx", axis=0, tiled=True)
    gate_part = jnp.einsum("red,edf->ref", portion, w_gate, preferred_element_type=jnp.float32)
    lifted = jnp.einsum("red,edf->ref", portion, w_up, preferred_element_type=jnp.float32)
    hidden = (jax.nn.silu(gate_part) * lifted).astype(jnp.bfloat16)
    summed = lax.psum_scatter(
        jnp.einsum("ref,efd->red", hidden, w_down, preferred_element_type=jnp.float32).astype(
            jnp.bfloat16
        ),
        "ctx",
        scatter_dimension=0,
        tiled=True,
    )
    result = summed.reshape(capacity, local_experts, exp_count, features)
    returned_rows = lax.all_to_all(result, "exp", split_axis=2, concat_axis=1, tiled=True).reshape(
        capacity * experts, features
    )
    routed = jnp.dot(placing.T, returned_rows, preferred_element_type=jnp.float32).astype(
        jnp.bfloat16
    )
    return (attended, routed)


def solution(mesh):
    in_specs = (
        P("ctx", "exp"),
        P("ctx", "exp"),
        P("ctx", "exp"),
        P(),
        P("ctx", None),
        P(),
        P(),
        P("exp", None, "ctx"),
        P("exp", None, "ctx"),
        P("exp", "ctx", None),
    )
    out_specs = (P("ctx", "exp"), P("ctx", "exp"))
    return jax.shard_map(
        per_device, mesh=mesh, in_specs=in_specs, out_specs=out_specs, check_vma=False
    )
```

profile of v0, /device:TPU:1, one launch (start us, length us, event | category | flops | bytes accessed | tf_op | source)
XLA Modules:
  0.0 716.0 jit_solution(13614119037769642773)
XLA Ops:
  8.0 1.5 copy.32
  13.1 1.6 fusion.81
  14.7 2.1 fusion.78
  16.8 2.1 fusion.79
  18.9 2.1 fusion.80
  21.0 4.4 compare_select_fusion.1
  25.4 35.9 %fusion.68 = s32[4096]{0:T(1024)S(1)} fusion(pred[4096]{0:T(1024)(128)(4,1)S(1)} %compare_reduce_fusion, pred[4096]{0:T(1024)(128)(4,1)S(1)} %compare_reduce_fusion.1, pred[4096]{0:T(1024)(128)(4,1)S(1)} %compare_reduce_fusion.2, pred[4096]{0:T(1024)(128)(4,1)S(1)} %compare_reduce_fusion.3, pred[4096]{0:T(1024)(128)(4,1)S(1)} %compare_reduce_fusion.4, ...), kind=kLoop, calls=%fused_computation.119 | loop fusion | flops 266240 | bytes 266468 | tf_op jit(solution)/shard_map/add | solution.py:23
  61.4 1.8 broadcast_compare_fusion
  67.5 28.0 %all-gather.4.cloned.1.call-done = bf16[4096,128]{1,0:T(8,128)(2,1)} async-done(((bf16[128,128]{1,0:T(8,128)(2,1)}), bf16[4096,128]{1,0:T(8,128)(2,1)}) %all-gather.4.cloned.1.call-update) | async-done | bytes 1048592 | tf_op jit(solution)/shard_map/all_gather | solution.py:28
  95.4 3.0 fusion.4
  98.4 4.0 copy-done.1
  102.4 2.5 fusion.5
  105.0 72.2 %all-gather.6.cloned.1.call-done = bf16[4096,128]{0,1:T(8,128)(2,1)} async-done(((bf16[128,128]{0,1:T(8,128)(2,1)}), bf16[4096,128]{0,1:T(8,128)(2,1)}) %all-gather.6.cloned.1.call-update) | async-done | bytes 1048592 | tf_op jit(solution)/shard_map/all_gather | solution.py:29
  177.2 7.1 multiply_reduce_fusion
  184.3 1.1 fusion.61
  185.4 15.2 %all-reduce = (f32[128,8]{0,1:T(8,128)S(1)}, f32[128]{0:T(128)S(1)}) all-reduce(f32[128,8]{0,1:T(8,128)S(1)} %fusion.61, f32[128]{0:T(128)S(1)} %get-tuple-element.78), channel_id=1, replica_groups=mesh['ctx'=32,'exp'=8] {'exp'}, use_global_device_ids=true, to_apply=%region_6.7 | all-reduce | flops 1152 | bytes 9216 | tf_op jit(solution)/shard_map/psum | solution.py:75
  201.1 13.5 %all_to_all.21 = bf16[32,8,640]{2,0,1:T(8,128)(2,1)S(1)} all-to-all(bf16[32,8,640]{2,0,1:T(8,128)(2,1)S(1)} %copy.36), channel_id=1, replica_groups=mesh['ctx'=32,'exp'=8] {'exp'}, dimensions={1} | all-to-all | bytes 655360 | tf_op jit(solution)/shard_map/all_to_all | solution.py:88
  215.9 172.5 %all-gather.8.cloned.1.call-done = bf16[1024,1,5120]{2,0,1:T(8,128)(2,1)} async-done(((bf16[32,1,5120]{2,0,1:T(8,128)(2,1)}), bf16[1024,1,5120]{2,0,1:T(8,128)(2,1)}) %all-gather.8.cloned.1.call-update) | async-done | bytes 10485776 | tf_op jit(solution)/shard_map/all_gather | solution.py:89
  388.4 8.6 %fusion.14 = f32[1024,1,256]{2,0,1:T(8,128)} fusion(bf16[1,5120,256]{2,1,0:T(8,128)(2,1)} %param.17, bf16[1024,1,5120]{2,0,1:T(8,128)(2,1)} %all-gather.8.cloned.1.call-done), kind=kOutput, calls=%fused_computation.16 | convolution fusion | flops 2684354560 | bytes 14155776 | tf_op jit(solution)/shard_map/red,edf->ref/dot_general | solution.py:90
  396.9 21.1 %convert_bitcast_fusion = bf16[1024,1,5120]{2,0,1:T(8,128)(2,1)} fusion(bf16[1,256,5120]{2,1,0:T(8,128)(2,1)S(1)} %copy-done, bf16[1,5120,256]{2,1,0:T(8,128)(2,1)} %param.18, bf16[1024,1,5120]{2,0,1:T(8,128)(2,1)} %all-gather.8.cloned.1.call-done, f32[1024,1,256]{2,0,1:T(8,128)} %fusion.14), kind=kOutput, calls=%fused_computation.5 | convolution fusion | flops 5375524864 | bytes 27262976 | tf_op jit(solution)/shard_map/ref,efd->red/dot_general | solution.py:94
  418.0 274.0 %reduce-scatter.2.cloned.1.call-done = bf16[32,1,5120]{2,0,1:T(8,128)(2,1)} async-done(((bf16[1024,1,5120]{2,0,1:T(8,128)(2,1)}), bf16[32,1,5120]{2,0,1:T(8,128)(2,1)}) %reduce-scatter.2.cloned.1.call-update) | async-done | bytes 327696 | tf_op jit(solution)/shard_map/reduce_scatter | solution.py:93
  692.0 1.7 copy.49
  693.7 4.8 all-to-all-start.1
  699.4 9.2 %all-to-all-done.1 = bf16[32,1,8,640]{3,0,1,2:T(8,128)(2,1)S(1)} async-done(((bf16[32,1,8,640]{3,0,1,2:T(8,128)(2,1)}), bf16[32,1,8,640]{3,0,1,2:T(8,128)(2,1)S(1)}, u32[]{:S(2)}, u32[]{:S(2)}) %all-to-all-start.1) | async-done | bytes 327712 | tf_op jit(solution)/shard_map/all_to_all | solution.py:102
  (89 shorter events, 12.2 us)
Async XLA Ops:
  7.2 389.8 %copy-start = (bf16[1,256,5120]{2,1,0:T(8,128)(2,1)S(1)}, bf16[1,256,5120]{2,1,0:T(8,128)(2,1)}, u32[]{:S(2)}) copy-start(bf16[1,256,5120]{2,1,0:T(8,128)(2,1)} %param.19) | copy-start | bytes 7864324
  7.2 88.3 %all-gather.4.cloned.1.call-start = ((), (), s32[]{:S(2)}) async-start(), calls=%async_computation.3 | async-start | bytes 1081344 | tf_op jit(solution)/shard_map/all_gather | solution.py:28
  7.9 169.3 %all-gather.6.cloned.1.call-start = ((), (), s32[]{:S(2)}) async-start(), calls=%async_computation.4 | async-start | bytes 1081344 | tf_op jit(solution)/shard_map/all_gather | solution.py:29
  9.5 378.9 %all-gather.8.cloned.1.call-start = ((), (), s32[]{:S(2)}) async-start(), calls=%async_computation.5 | async-start | bytes 10813440 | tf_op jit(solution)/shard_map/all_gather | solution.py:89
  98.4 4.0 copy-start.1
  104.9 95.7 %copy-start.2 = (s32[128,1]{0,1:T(1,128)S(1)}, s32[128,1]{0,1:T(1,128)}, u32[]{:S(2)}) copy-start(s32[128,1]{0,1:T(1,128)} %param.14) | copy-start | bytes 1540
  215.6 476.4 %reduce-scatter.2.cloned.1.call-start = ((), (), s32[]{:S(2)}) async-start(), calls=%async_computation.6 | async-start | bytes 10813440 | tf_op jit(solution)/shard_map/reduce_scatter | solution.py:93
  693.7 14.8 %all-to-all-start.1 = ((bf16[32,1,8,640]{3,0,1,2:T(8,128)(2,1)}), bf16[32,1,8,640]{3,0,1,2:T(8,128)(2,1)S(1)}, u32[]{:S(2)}, u32[]{:S(2)}) async-start(bf16[32,1,8,640]{3,0,1,2:T(8,128)(2,1)} %bitcast.191), calls=%async_computation.2 | async-start | bytes 655360 | tf_op jit(solution)/shard_map/all_to_all | solution.py:102
Sparse Core Ops, SparseCore 0:
  11.4 83.9 all-gather.3
  99.2 77.9 all-gather.5
  215.7 172.5 all-gather.7
  418.1 273.8 reduce-scatter.1
where the time goes:
time: 717 us; the launch traced here: 716 us
  waiting for transfers between devices  557 us (78%)
  other arithmetic  50.5 us (7%)
  matrix products  42.1 us (6%)
  blocking collectives  28.7 us (4%)
  local copies, waits for them, and re-layouts  19 us (3%)
  between operations  13.9 us (2%)
    reduce_scatter x1, waiting for transfers between devices, per_device(): lax.psum_scatter(jnp.einsum('ref,efd->red', hidden, w_down, preferred_ele...  274 us
    all_gather x1, waiting for transfers between devices, per_device(): portion = lax.all_gather(arrived, 'ctx', axis=0, tiled=True)  172 us
    all_gather x1, waiting for transfers between devices, per_device(): value_piece = lax.all_gather(values, 'ctx', axis=0, tiled=True)  72.2 us
    add x1, other arithmetic, per_device(): block_order[everywhere // half_rows] * half_rows + everywhere % half_rows  35.9 us
    all_gather x1, waiting for transfers between devices, per_device(): key_piece = lax.all_gather(keys, 'ctx', axis=0, tiled=True)  28 us
    dot_general x1, matrix products, per_device(): jnp.einsum('ref,efd->red', hidden, w_down, preferred_element_type=jnp.flo...  21.1 us
    psum x1, blocking collectives, per_device(): lax.psum((jnp.sum(values_f32 * values_f32, axis=1), jnp.dot(scaled, route...  15.2 us
  transfers between devices with their start and end apart: 5, of which 5 were waited for; matrix products, arithmetic and copies ran while one was open for 9% of the time, Pallas kernels for 0%

commit v1 on v0

v1 whole, which is shorter than its diff:
```python
import functools
import math

import jax
import jax.numpy as jnp
from jax import lax
from jax.experimental import pallas as pl
from jax.experimental.pallas import tpu as pltpu
from jax.sharding import PartitionSpec as P

HEAD_DIM = 128
CAP = 32
MESH = pl.DeviceIdType.MESH

PLANES = 2
SIDE = 4
EXPERTS = 8
WIDTH = 5120
CHUNK = WIDTH // EXPERTS
HALF = CAP // 2
PIECE_COLS = WIDTH // 2
GROUP = SIDE * SIDE * HALF
HID = 256


def mod4(v):
    return lax.rem(v + 2 * SIDE, SIDE)


class Torus:
    def __init__(self, h, plane, y, x, e):
        self.h, self.plane, self.y, self.x, self.e = h, plane, y, x, e

    def at(self, dp, dq):
        if self.h == 0:
            return mod4(self.y + dq), mod4(self.x + dp)
        return mod4(self.y + dp), mod4(self.x + dq)

    def rows(self, dp, dq):
        y, x = self.at(dp, dq)
        return pl.ds(pl.multiple_of((y * SIDE + x) * HALF, HALF), HALF)

    def dev(self, dp, dq):
        y, x = self.at(dp, dq)
        return (self.plane * SIDE * SIDE + y * SIDE + x, self.e)


def moe_kernel(
    att_ref,
    routes_ref,
    gain_ref,
    router_ref,
    wg_hbm,
    wu_hbm,
    wd_hbm,
    out_ref,
    wg,
    wu,
    wd,
    pack,
    xin,
    g,
    part,
    ru1,
    ru2,
    rv1,
    rv2,
    fin,
    ret,
    acc,
    hid,
    w_sem,
    a2a_s,
    a2a_r,
    ag_s,
    ag_r,
    rs_s,
    rs_r,
    back_s,
    back_r,
):
    ctx = lax.axis_index("ctx")
    e = lax.axis_index("exp")
    plane = ctx // (SIDE * SIDE)
    other = 1 - plane
    spot = lax.rem(ctx, SIDE * SIDE)
    y, x = spot // SIDE, lax.rem(spot, SIDE)
    tori = [Torus(h, plane, y, x, e) for h in range(2)]
    planes = (plane, other)
    sent = []

    def send(src, dst, ssem, rsem, dev):
        copy = pltpu.make_async_remote_copy(
            src_ref=src, dst_ref=dst, send_sem=ssem, recv_sem=rsem, device_id=dev, device_id_type=MESH
        )
        copy.start()
        sent.append(copy)

    def arrived(dst, ssem, rsem):
        pltpu.make_async_remote_copy(
            src_ref=dst, dst_ref=dst, send_sem=ssem, recv_sem=rsem, device_id=tori[0].dev(1, 0), device_id_type=MESH
        ).wait_recv()

    def column(pl_index, d):
        return (pl_index * SIDE * SIDE + spot, lax.rem(e + d, EXPERTS))

    barrier = pltpu.get_barrier_semaphore()
    partners = [column(plane, d) for d in range(1, EXPERTS)]
    partners += [column(other, d) for d in range(EXPERTS)]
    partners += [tori[0].dev(1, 0), tori[0].dev(-1, 0), tori[0].dev(0, 1), tori[0].dev(0, -1)]
    for dev in partners:
        pl.semaphore_signal(barrier, inc=1, device_id=dev, device_id_type=MESH)

    loads = [
        pltpu.make_async_copy(wg_hbm, wg, w_sem.at[0]),
        pltpu.make_async_copy(wu_hbm, wu, w_sem.at[1]),
        pltpu.make_async_copy(wd_hbm, wd, w_sem.at[2]),
    ]
    for load in loads:
        load.start()

    n_rows = att_ref.shape[0]
    onehot = (lax.broadcasted_iota(jnp.int32, (EXPERTS, n_rows), 0) == routes_ref[...]).astype(jnp.float32)
    before = (
        lax.broadcasted_iota(jnp.int32, (n_rows, n_rows), 0)
        < lax.broadcasted_iota(jnp.int32, (n_rows, n_rows), 1)
    ).astype(jnp.bfloat16)
    earlier = jnp.dot(onehot.astype(jnp.bfloat16), before, preferred_element_type=jnp.float32)
    code = jnp.sum(onehot * earlier, axis=0, keepdims=True).astype(jnp.int32) + routes_ref[...] * CAP
    placing = (lax.broadcasted_iota(jnp.int32, (EXPERTS * CAP, n_rows), 0) == code).astype(jnp.bfloat16)
    packed = jnp.dot(placing, att_ref[...], preferred_element_type=jnp.float32).astype(jnp.bfloat16)
    pack[...] = packed.reshape(EXPERTS, CAP, CHUNK)

    pl.semaphore_wait(barrier, len(partners))

    for w in range(PLANES):
        for d in range(1 - w, EXPERTS):
            to = lax.rem(e + d, EXPERTS)
            send(
                pack.at[to],
                xin.at[w, e],
                a2a_s.at[w, d],
                a2a_r.at[w, d],
                column(planes[w], d),
            )
    own = pltpu.make_async_copy(pack.at[e], xin.at[0, e], a2a_s.at[0, 0])
    own.start()

    def norm(w):
        for d in range(1 - w, EXPERTS):
            src = lax.rem(e - d + EXPERTS, EXPERTS)
            arrived(xin.at[w, src], a2a_s.at[w, d], a2a_r.at[w, d])
        if w == 0:
            own.wait()
        squares = jnp.zeros((CAP, 1), jnp.float32)
        for j in range(EXPERTS):
            v = xin[w, j].astype(jnp.float32)
            squares += jnp.sum(v * v, axis=1, keepdims=True)
        inverse = lax.rsqrt(squares / WIDTH + 1e-05)
        logits = jnp.zeros((CAP, EXPERTS), jnp.float32)
        for j in range(EXPERTS):
            cols = pl.ds(j * CHUNK, CHUNK)
            v = xin[w, j].astype(jnp.float32) * inverse * gain_ref[:, cols]
            logits += jnp.dot(
                v, router_ref[cols, :], precision=lax.Precision.HIGHEST, preferred_element_type=jnp.float32
            )
        mine = lax.broadcasted_iota(jnp.int32, logits.shape, 1) == e
        logit = jnp.sum(jnp.where(mine, logits, 0.0), axis=1, keepdims=True)
        gate = 1.0 / (1.0 + jnp.exp(-logit))
        for j in range(EXPERTS):
            cols = pl.ds(j * CHUNK, CHUNK)
            v = xin[w, j].astype(jnp.float32) * inverse * gain_ref[:, cols]
            v = (v * gate).astype(jnp.bfloat16)
            for t in tori:
                g[w, t.h, t.rows(0, 0), cols] = v[t.h * HALF : (t.h + 1) * HALF]

    left_half, right_half = pl.ds(0, PIECE_COLS), pl.ds(PIECE_COLS, PIECE_COLS)
    OFFS = (0, -1, 1, 2)

    def ag_second(w, t, i):
        piece = g.at[w, t.h, t.rows(OFFS[i], 0)]
        for s, dq in ((0, 1), (1, -1)):
            n = 4 + 2 * i + s
            send(piece, piece, ag_s.at[w, t.h, n], ag_r.at[w, t.h, n], t.dev(0, dq))

    def ag_second_arrived(w, t, i, s):
        n = 4 + 2 * i + s
        arrived(g.at[w, t.h, t.rows(OFFS[i], -1 if s == 0 else 1)], ag_s.at[w, t.h, n], ag_r.at[w, t.h, n])

    def ag_start(w):
        for t in tori:
            piece = g.at[w, t.h, t.rows(0, 0)]
            for s, dp in ((0, 1), (1, -1)):
                send(piece, piece, ag_s.at[w, t.h, s], ag_r.at[w, t.h, s], t.dev(dp, 0))
        for t in tori:
            ag_second(w, t, 0)

    def ag_near(w):
        for t in tori:
            for s, dp, cols in ((0, -1, left_half), (1, 1, right_half)):
                arrived(g.at[w, t.h, t.rows(dp, 0)], ag_s.at[w, t.h, s], ag_r.at[w, t.h, s])
                part_of = g.at[w, t.h, t.rows(dp, 0), cols]
                send(part_of, part_of, ag_s.at[w, t.h, 2 + s], ag_r.at[w, t.h, 2 + s], t.dev(-dp, 0))
        for t in tori:
            ag_second(w, t, 1)
            ag_second(w, t, 2)

    def ag_far(w):
        for t in tori:
            for s, cols in ((0, left_half), (1, right_half)):
                arrived(g.at[w, t.h, t.rows(2, 0), cols], ag_s.at[w, t.h, 2 + s], ag_r.at[w, t.h, 2 + s])
            ag_second(w, t, 3)

    OPPOSITE = ((0, 0), (1, 1), (2, 1), (3, 0))

    def ag_forward(w, i):
        s = OPPOSITE[i][1]
        dq = 1 if s == 0 else -1
        for t in tori:
            ag_second_arrived(w, t, i, s)
            piece = g.at[w, t.h, t.rows(OFFS[i], -dq)]
            send(piece, piece, ag_s.at[w, t.h, 12 + i], ag_r.at[w, t.h, 12 + i], t.dev(0, dq))

    def ag_done(w, t):
        for i in range(4):
            ag_second_arrived(w, t, i, 1 - OPPOSITE[i][1])
            arrived(g.at[w, t.h, t.rows(OFFS[i], 2)], ag_s.at[w, t.h, 12 + i], ag_r.at[w, t.h, 12 + i])

    def ffn(w, h):
        step = 1280
        acc[...] = jnp.zeros_like(acc)

        @pl.loop(0, WIDTH // step)
        def _(k):
            cols = pl.ds(pl.multiple_of(k * step, step), step)
            rows = g[w, h, :, cols]
            acc[0] += jnp.dot(rows, wg[cols, :], preferred_element_type=jnp.float32)
            acc[1] += jnp.dot(rows, wu[cols, :], preferred_element_type=jnp.float32)

        v = acc[0]
        hid[...] = (v / (1.0 + jnp.exp(-v)) * acc[1]).astype(jnp.bfloat16)
        wide = 512

        @pl.loop(0, WIDTH // wide)
        def _(k):
            cols = pl.ds(pl.multiple_of(k * wide, wide), wide)
            part[w, h, :, cols] = jnp.dot(hid[...], wd[:, cols], preferred_element_type=jnp.float32).astype(
                jnp.bfloat16
            )

    def add(ref, *more):
        total = ref[...].astype(jnp.float32)
        for m in more:
            total = total + m[...].astype(jnp.float32)
        ref[...] = total.astype(jnp.bfloat16)

    def rs_start(w):
        for t in tori:
            for i, s in OPPOSITE:
                send(
                    part.at[w, t.h, t.rows(OFFS[i], 2)],
                    ru1.at[w, t.h, i],
                    rs_s.at[w, t.h, i],
                    rs_r.at[w, t.h, i],
                    t.dev(0, 1 if s == 0 else -1),
                )

    def rs_second(w, t, i, s):
        n = 4 + 2 * i + s
        dq = 1 if s == 0 else -1
        send(
            part.at[w, t.h, t.rows(OFFS[i], dq)],
            ru2.at[w, t.h, i, s],
            rs_s.at[w, t.h, n],
            rs_r.at[w, t.h, n],
            t.dev(0, dq),
        )

    def rs_plain(w):
        for t in tori:
            for i, s in OPPOSITE:
                rs_second(w, t, i, 1 - s)

    def rs_joined(w, i):
        s = OPPOSITE[i][1]
        dq = 1 if s == 0 else -1
        for t in tori:
            arrived(ru1.at[w, t.h, i], rs_s.at[w, t.h, i], rs_r.at[w, t.h, i])
            add(part.at[w, t.h, t.rows(OFFS[i], dq)], ru1.at[w, t.h, i])
            rs_second(w, t, i, s)

    def rs_sum(w, t, i):
        for s in range(2):
            n = 4 + 2 * i + s
            arrived(ru2.at[w, t.h, i, s], rs_s.at[w, t.h, n], rs_r.at[w, t.h, n])
        add(part.at[w, t.h, t.rows(OFFS[i], 0)], ru2.at[w, t.h, i, 0], ru2.at[w, t.h, i, 1])

    def rs_turn(w):
        for t in tori:
            rs_sum(w, t, 3)
            for s, dp, cols in ((0, 1, left_half), (1, -1, right_half)):
                send(
                    part.at[w, t.h, t.rows(2, 0), cols],
                    rv1.at[w, t.h, s],
                    rs_s.at[w, t.h, 12 + s],
                    rs_r.at[w, t.h, 12 + s],
                    t.dev(dp, 0),
                )
        for t in tori:
            for i in (1, 2):
                rs_sum(w, t, i)

    def rs_last(w):
        for t in tori:
            for s, dp, cols in ((0, 1, left_half), (1, -1, right_half)):
                arrived(rv1.at[w, t.h, s], rs_s.at[w, t.h, 12 + s], rs_r.at[w, t.h, 12 + s])
                add(part.at[w, t.h, t.rows(dp, 0), cols], rv1.at[w, t.h, s])
                send(
                    part.at[w, t.h, t.rows(dp, 0)],
                    rv2.at[w, t.h, s],
                    rs_s.at[w, t.h, 14 + s],
                    rs_r.at[w, t.h, 14 + s],
                    t.dev(dp, 0),
                )
        for t in tori:
            rs_sum(w, t, 0)

    def rs_finish(w):
        for t in tori:
            for s in range(2):
                arrived(rv2.at[w, t.h, s], rs_s.at[w, t.h, 14 + s], rs_r.at[w, t.h, 14 + s])
            for j in range(EXPERTS):
                cols = pl.ds(j * CHUNK, CHUNK)
                total = part[w, t.h, t.rows(0, 0), cols].astype(jnp.float32)
                for s in range(2):
                    total = total + rv2[w, t.h, s, :, cols].astype(jnp.float32)
                fin[w, j, pl.ds(t.h * HALF, HALF)] = total.astype(jnp.bfloat16)

    def back(w):
        for d in range(1 - w, EXPERTS):
            to = lax.rem(e + d, EXPERTS)
            send(fin.at[w, to], ret.at[w, e], back_s.at[w, d], back_r.at[w, d], column(planes[w], d))

    ag = ag_start
    norm(0)
    ag(0)
    norm(1)
    ag_near(0)
    ag_far(0)
    ag(1)
    ag_forward(0, 0)
    ag_forward(0, 1)
    ag_near(1)
    ag_forward(0, 2)
    ag_forward(0, 3)
    ag_far(1)
    for load in loads:
        load.wait()
    ag_done(0, tori[0])
    ag_done(0, tori[1])
    ag_forward(1, 0)
    ag_forward(1, 1)
    ffn(0, 0)
    ag_forward(1, 2)
    ag_forward(1, 3)
    ffn(0, 1)
    rs_start(0)
    rs_plain(0)
    ag_done(1, tori[0])
    ag_done(1, tori[1])
    for i in range(4):
        rs_joined(0, i)
    ffn(1, 0)
    ffn(1, 1)
    rs_start(1)
    rs_plain(1)
    rs_turn(0)
    for i in range(4):
        rs_joined(1, i)
    rs_last(0)
    rs_finish(0)
    back(0)
    rs_turn(1)
    rs_last(1)
    rs_finish(1)
    back(1)
    mine = pltpu.make_async_copy(fin.at[0, e], ret.at[0, e], back_s.at[0, 0])
    mine.start()

    routed = None
    for w in range(PLANES):
        for d in range(1 - w, EXPERTS):
            src = lax.rem(e - d + EXPERTS, EXPERTS)
            arrived(ret.at[w, src], back_s.at[w, d], back_r.at[w, d])
        if w == 0:
            mine.wait()
        rows = ret[w].reshape(EXPERTS * CAP, CHUNK)
        term = lax.dot_general(
            placing, rows, (((0,), (0,)), ((), ())), preferred_element_type=jnp.float32
        )
        routed = term if routed is None else routed + term
    out_ref[...] = routed.astype(jnp.bfloat16)
    for copy in sent:
        copy.wait_send()


def moe(attended, routes, norm_gain, router, w_gate, w_up, w_down):
    vmem = pl.BlockSpec(memory_space=pltpu.VMEM)
    anywhere = pl.BlockSpec(memory_space=pl.ANY)
    bf16, f32 = jnp.bfloat16, jnp.float32
    dma = pltpu.SemaphoreType.DMA
    return pl.pallas_call(
        moe_kernel,
        out_shape=jax.ShapeDtypeStruct(attended.shape, bf16),
        in_specs=[vmem, vmem, vmem, vmem, anywhere, anywhere, anywhere],
        out_specs=vmem,
        scratch_shapes=[
            pltpu.VMEM((WIDTH, HID), bf16),
            pltpu.VMEM((WIDTH, HID), bf16),
            pltpu.VMEM((HID, WIDTH), bf16),
            pltpu.VMEM((EXPERTS, CAP, CHUNK), bf16),
            pltpu.VMEM((PLANES, EXPERTS, CAP, CHUNK), bf16),
            pltpu.VMEM((PLANES, 2, GROUP, WIDTH), bf16),
            pltpu.VMEM((PLANES, 2, GROUP, WIDTH), bf16),
            pltpu.VMEM((PLANES, 2, 4, HALF, WIDTH), bf16),
            pltpu.VMEM((PLANES, 2, 4, 2, HALF, WIDTH), bf16),
            pltpu.VMEM((PLANES, 2, 2, HALF, PIECE_COLS), bf16),
            pltpu.VMEM((PLANES, 2, 2, HALF, WIDTH), bf16),
            pltpu.VMEM((PLANES, EXPERTS, CAP, CHUNK), bf16),
            pltpu.VMEM((PLANES, EXPERTS, CAP, CHUNK), bf16),
            pltpu.VMEM((2, GROUP, HID), f32),
            pltpu.VMEM((GROUP, HID), bf16),
            dma((3,)),
            dma((PLANES, EXPERTS)),
            dma((PLANES, EXPERTS)),
            dma((PLANES, 2, 16)),
            dma((PLANES, 2, 16)),
            dma((PLANES, 2, 16)),
            dma((PLANES, 2, 16)),
            dma((PLANES, EXPERTS)),
            dma((PLANES, EXPERTS)),
        ],
        compiler_params=pltpu.CompilerParams(
            collective_id=1, has_side_effects=True, vmem_limit_bytes=62 << 20
        ),
        name="experts",
    )(
        attended,
        routes.reshape(1, -1),
        norm_gain.reshape(1, -1),
        router,
        w_gate[0],
        w_up[0],
        w_down[0],
    )


def per_device(queries, keys, values, block_order, routes, norm_gain, router, w_gate, w_up, w_down):
    rows_here = queries.shape[0]
    ctx_index = lax.axis_index("ctx")
    kv_local = keys.shape[1] // HEAD_DIM
    q_local = queries.shape[1] // HEAD_DIM
    per_group = q_local // kv_local
    half_rows = rows_here // 2
    position = (block_order[:, None] * half_rows + jnp.arange(half_rows, dtype=jnp.int32)[None, :]).reshape(-1)
    query_pos = lax.dynamic_slice_in_dim(position, ctx_index * rows_here, rows_here)
    grouped = queries.reshape(rows_here, kv_local, per_group, HEAD_DIM)
    score_scale = 1.0 / math.sqrt(HEAD_DIM)
    key_piece = lax.all_gather(keys, "ctx", axis=0, tiled=True)
    value_piece = lax.all_gather(values, "ctx", axis=0, tiled=True)
    piece_rows = key_piece.shape[0]
    scores = (
        jnp.einsum(
            "sgqd,rgd->gqsr",
            grouped,
            key_piece.reshape(piece_rows, kv_local, HEAD_DIM),
            preferred_element_type=jnp.float32,
        )
        * score_scale
    )
    allowed = position[None, :] <= query_pos[:, None]
    scores = jnp.where(allowed, scores, -1e30)
    newest_max = jnp.max(scores, axis=3)
    weights = jnp.where(allowed, jnp.exp(scores - newest_max[..., None]), 0.0)
    running_sum = jnp.sum(weights, axis=3)
    weighted = jnp.einsum(
        "gqsr,rgd->gqsd",
        weights.astype(jnp.bfloat16),
        value_piece.reshape(piece_rows, kv_local, HEAD_DIM),
        preferred_element_type=jnp.float32,
    )
    attended = (
        (weighted / running_sum[..., None])
        .transpose(2, 0, 1, 3)
        .reshape(rows_here, q_local * HEAD_DIM)
    )
    attended = attended.astype(jnp.bfloat16)
    routed = moe(attended, routes, norm_gain, router, w_gate, w_up, w_down)
    return (attended, routed)


def solution(mesh):
    in_specs = (
        P("ctx", "exp"),
        P("ctx", "exp"),
        P("ctx", "exp"),
        P(),
        P("ctx", None),
        P(),
        P(),
        P("exp", None, "ctx"),
        P("exp", None, "ctx"),
        P("exp", "ctx", None),
    )
    out_specs = (P("ctx", "exp"), P("ctx", "exp"))
    return jax.shard_map(
        per_device, mesh=mesh, in_specs=in_specs, out_specs=out_specs, check_vma=False
    )
```

time: 717 us -> 345 us (0.48)
  waiting for transfers between devices: 557 us -> 152 us
  Pallas kernels: 0 us -> 150 us
  other arithmetic: 50.5 us -> 5.12 us
  matrix products: 42.1 us -> 9.97 us
  blocking collectives: 28.7 us -> 0 us
    reduce_scatter x1 -> x0, waiting for transfers between devices: 274 us -> none  [per_device(): lax.psum_scatter(jnp.einsum('ref,efd->red', hidden, w_down, preferred_ele...]
    all_gather x1 -> x0, waiting for transfers between devices: 172 us -> none  [per_device(): portion = lax.all_gather(arrived, 'ctx', axis=0, tiled=True)]
    pallas_call x0 -> x1, Pallas kernels: none -> 150 us  [moe(): pl.pallas_call(moe_kernel, out_shape=jax.ShapeDtypeStruct(attended.shape,...]
    all_gather x1, waiting for transfers between devices: 28 us -> 79 us  [per_device(): key_piece = lax.all_gather(keys, 'ctx', axis=0, tiled=True)]
    add x2 -> x1, other arithmetic: 36.6 us -> 0.07 us  [per_device(): block_order[:, None] * half_rows]
    dot_general x5 -> x0, matrix products: 32 us -> none  [the longest x1 21.1 us: per_device(): jnp.einsum('ref,efd->red', hidden, w_down, preferred_element_type=jnp.flo...]
    psum x1 -> x0, blocking collectives: 15.2 us -> none  [per_device(): lax.psum((jnp.sum(values_f32 * values_f32, axis=1), jnp.dot(scaled, route...]
    all_to_all x1 -> x0, blocking collectives: 13.5 us -> none  [per_device(): lax.all_to_all(outbound, 'exp', split_axis=1, concat_axis=2, tiled=True)]
  transfers between devices with their start and end apart: 5 -> 2, of which waited for: 5 -> 2; matrix products, arithmetic and copies ran while one was open for 9% -> 4% of each run, Pallas kernels for 0% -> 0%
where the time goes in v1:
time: 345 us; the launch traced here: 343 us
  waiting for transfers between devices  152 us (44%)
  Pallas kernels  150 us (43%)
  between operations  14.1 us (4%)
  local copies, waits for them, and re-layouts  12.3 us (4%)
  matrix products  9.97 us (3%)
  other arithmetic  5.12 us (1%)
    pallas_call x1, Pallas kernels, moe(): pl.pallas_call(moe_kernel, out_shape=jax.ShapeDtypeStruct(attended.shape,...  150 us
    all_gather x1, waiting for transfers between devices, per_device(): key_piece = lax.all_gather(keys, 'ctx', axis=0, tiled=True)  79 us
    all_gather x1, waiting for transfers between devices, per_device(): value_piece = lax.all_gather(values, 'ctx', axis=0, tiled=True)  72.3 us
    unnamed x7, local copies, waits for them, and re-layouts  12.1 us
    dot_general x1, matrix products, per_device(): jnp.einsum('gqsr,rgd->gqsd', weights.astype(jnp.bfloat16), value_piece.re...  7.01 us
  transfers between devices with their start and end apart: 2, of which 2 were waited for; matrix products, arithmetic and copies ran while one was open for 4% of the time, Pallas kernels for 0%

profile of v1, /device:TPU:1, one launch (start us, length us, event | category | flops | bytes accessed | tf_op | source)
XLA Modules:
  0.0 343.4 jit_solution(10143313918499787343)
XLA Ops:
  7.2 0.0 all-gather.3.cloned.1.call-start
  7.2 0.7 all-gather.3.cloned.1.call-update
  7.9 0.0 all-gather.5.cloned.1.call-start
  7.9 1.5 copy.19
  9.4 0.0 all-gather.5.cloned.1.call-update
  9.4 0.7 broadcast_multiply_fusion
  10.1 0.1 iota_add_fusion
  10.2 0.1 add.27
  10.3 1.1 copy.17
  11.3 3.2 copy.22.router_ref
  14.5 0.1 dynamic_slice.3
  14.6 1.8 broadcast_compare_fusion
  16.4 79.0 %all-gather.3.cloned.1.call-done = bf16[4096,128]{1,0:T(8,128)(2,1)} async-done(((bf16[128,128]{1,0:T(8,128)(2,1)}), bf16[4096,128]{1,0:T(8,128)(2,1)}) %all-gather.3.cloned.1.call-update) | async-done | bytes 1048592 | tf_op jit(solution)/shard_map/all_gather | solution.py:469
  95.4 3.0 fusion
  98.4 0.0 copy-start
  98.4 4.0 %copy-done = f32[4096,128,5]{1,0,2:T(8,128)} copy-done((f32[4096,128,5]{1,0,2:T(8,128)}, f32[4096,128,5]{1,0,2:T(8,128)S(1)}, u32[]{:S(2)}) %copy-start) | copy-done | bytes 10485784
  102.3 2.5 fusion.1
  104.9 72.3 %all-gather.5.cloned.1.call-done = bf16[4096,128]{0,1:T(8,128)(2,1)} async-done(((bf16[128,128]{0,1:T(8,128)(2,1)}), bf16[4096,128]{0,1:T(8,128)(2,1)}) %all-gather.5.cloned.1.call-update) | async-done | bytes 1048592 | tf_op jit(solution)/shard_map/all_gather | solution.py:470
  177.2 7.0 %fusion.10 = bf16[5,128,128]{1,2,0:T(8,128)(2,1)S(1)} fusion(f32[4096,128,5]{1,0,2:T(8,128)} %copy-done, f32[5,128]{1,0:T(8,128)S(1)} %get-tuple-element.4, pred[128,4096]{0,1:T(8,128)(4,1)S(1)} %broadcast_compare_fusion, bf16[4096,128]{0,1:T(8,128)(2,1)} %all-gather.5.cloned.1.call-done, f32[5,128]{1,0:T(8,128)S(1)} %fusion.1), kind=kOutput, calls=%fused_computation.9 | convolution fusion | flops 684359680 | bytes 12227584 | tf_op jit(solution)/shard_map/gqsr,rgd->gqsd/dot_general | solution.py:486
  184.2 0.8 copy.23.att_ref
  185.0 150.0 %experts.1 = bf16[128,640]{1,0:T(8,128)(2,1)} custom-call(bf16[128,640]{1,0:T(8,128)(2,1)} %copy.23.att_ref, s32[1,128]{1,0:T(1,128)} %bitcast.52, f32[1,5120]{1,0:T(1,128)} %bitcast.51, f32[5120,8]{1,0:T(8,128)} %copy.22.router_ref, bf16[5120,256]{1,0:T(8,128)(2,1)} %bitcast.46, bf16[5120,256]{1,0:T(8,128)(2,1)} %bitcast.47, bf16[256,5120]{1,0:T(8,128)(2,1)} %bitcast.48), custom_call_target="tpu_custom_call" | custom-call | tf_op jit(solution)/shard_map/experts/pallas_call | solution.py:412
  335.0 1.6 copy.27
Async XLA Ops:
  7.2 88.2 %all-gather.3.cloned.1.call-start = ((), (), s32[]{:S(2)}) async-start(), calls=%async_computation | async-start | bytes 1081344 | tf_op jit(solution)/shard_map/all_gather | solution.py:469
  7.9 169.3 %all-gather.5.cloned.1.call-start = ((), (), s32[]{:S(2)}) async-start(), calls=%async_computation.1 | async-start | bytes 1081344 | tf_op jit(solution)/shard_map/all_gather | solution.py:470
  98.4 4.0 %copy-start = (f32[4096,128,5]{1,0,2:T(8,128)}, f32[4096,128,5]{1,0,2:T(8,128)S(1)}, u32[]{:S(2)}) copy-start(f32[4096,128,5]{1,0,2:T(8,128)S(1)} %get-tuple-element.5) | copy-start | bytes 31457284
Sparse Core Ops, SparseCore 0:
  11.4 83.9 all-gather.2
  99.2 77.9 all-gather.4

commit v2 on v1

--- a/solution.py
+++ b/solution.py
@@ -27,6 +27,65 @@
     return lax.rem(v + 2 * SIDE, SIDE)
 
 
+OFFS = (0, -1, 1, 2)
+OPPOSITE = ((0, 0), (1, 1), (2, 1), (3, 0))
+
+
+class Gather:
+    def __init__(self, tori, piece, half, ssem, rsem, send, arrived):
+        self.tori, self.piece, self.half = tori, piece, half
+        self.ssem, self.rsem, self.send, self.arrived = ssem, rsem, send, arrived
+
+    def sems(self, t, n):
+        return self.ssem.at[t.h, n], self.rsem.at[t.h, n]
+
+    def second(self, t, i):
+        piece = self.piece(t, OFFS[i], 0)
+        for s, dq in ((0, 1), (1, -1)):
+            self.send(piece, piece, *self.sems(t, 4 + 2 * i + s), t.dev(0, dq))
+
+    def second_arrived(self, t, i, s):
+        self.arrived(self.piece(t, OFFS[i], -1 if s == 0 else 1), *self.sems(t, 4 + 2 * i + s))
+
+    def start(self):
+        for t in self.tori:
+            piece = self.piece(t, 0, 0)
+            for s, dp in ((0, 1), (1, -1)):
+                self.send(piece, piece, *self.sems(t, s), t.dev(dp, 0))
+        for t in self.tori:
+            self.second(t, 0)
+
+    def near(self):
+        for t in self.tori:
+            for s, dp in ((0, -1), (1, 1)):
+                self.arrived(self.piece(t, dp, 0), *self.sems(t, s))
+                half = self.half(t, dp, 0, s)
+                self.send(half, half, *self.sems(t, 2 + s), t.dev(-dp, 0))
+        for t in self.tori:
+            self.second(t, 1)
+            self.second(t, 2)
+
+    def far(self):
+        for t in self.tori:
+            for s in range(2):
+                self.arrived(self.half(t, 2, 0, s), *self.sems(t, 2 + s))
+            self.second(t, 3)
+
+    def forward(self, i):
+        s = OPPOSITE[i][1]
+        dq = 1 if s == 0 else -1
+        for t in self.tori:
+            self.second_arrived(t, i, s)
+            piece = self.piece(t, OFFS[i], -dq)
+            self.send(piece, piece, *self.sems(t, 12 + i), t.dev(0, dq))
+
+    def done(self):
+        for t in self.tori:
+            for i in range(4):
+                self.second_arrived(t, i, 1 - OPPOSITE[i][1])
+                self.arrived(self.piece(t, OFFS[i], 2), *self.sems(t, 12 + i))
+
+
 class Torus:
     def __init__(self, h, plane, y, x, e):
         self.h, self.plane, self.y, self.x, self.e = h, plane, y, x, e
@@ -36,24 +95,32 @@
             return mod4(self.y + dq), mod4(self.x + dp)
         return mod4(self.y + dp), mod4(self.x + dq)
 
-    def rows(self, dp, dq):
+    def rows(self, dp, dq, n=HALF, first=0, count=None):
         y, x = self.at(dp, dq)
-        return pl.ds(pl.multiple_of((y * SIDE + x) * HALF, HALF), HALF)
+        return pl.ds(pl.multiple_of((y * SIDE + x) * n + first, HALF), count or n)
 
     def dev(self, dp, dq):
         y, x = self.at(dp, dq)
         return (self.plane * SIDE * SIDE + y * SIDE + x, self.e)
 
 
-def moe_kernel(
-    att_ref,
+def kernel(
+    q_ref,
+    k_ref,
+    v_ref,
+    order_ref,
     routes_ref,
     gain_ref,
     router_ref,
     wg_hbm,
     wu_hbm,
     wd_hbm,
+    att_ref,
     out_ref,
+    kv,
+    soft_max,
+    soft_sum,
+    soft_acc,
     wg,
     wu,
     wd,
@@ -70,6 +137,10 @@
     acc,
     hid,
     w_sem,
+    z_s,
+    z_r,
+    kv_s,
+    kv_r,
     a2a_s,
     a2a_r,
     ag_s,
@@ -128,10 +199,102 @@
     earlier = jnp.dot(onehot.astype(jnp.bfloat16), before, preferred_element_type=jnp.float32)
     code = jnp.sum(onehot * earlier, axis=0, keepdims=True).astype(jnp.int32) + routes_ref[...] * CAP
     placing = (lax.broadcasted_iota(jnp.int32, (EXPERTS * CAP, n_rows), 0) == code).astype(jnp.bfloat16)
+
+    n = n_rows
+    kv[0, 0, tori[0].rows(0, 0, n)] = k_ref[...]
+    kv[0, 1, tori[1].rows(0, 0, n)] = v_ref[...]
+    soft_max[...] = jnp.full_like(soft_max, -1e30)
+    soft_sum[...] = jnp.zeros_like(soft_sum)
+    soft_acc[...] = jnp.zeros_like(soft_acc)
+    pl.semaphore_wait(barrier, len(partners))
+
+    kv_gather = [
+        Gather(
+            tori,
+            lambda t, dp, dq, w=w: kv.at[w, t.h, t.rows(dp, dq, n)],
+            lambda t, dp, dq, s, w=w: kv.at[w, t.h, t.rows(dp, dq, n, s * (n // 2), n // 2)],
+            kv_s.at[w],
+            kv_r.at[w],
+            send,
+            arrived,
+        )
+        for w in range(PLANES)
+    ]
+    for t in tori:
+        send(
+            kv.at[0, t.h, t.rows(0, 0, n)],
+            kv.at[1, t.h, t.rows(0, 0, n)],
+            z_s.at[t.h],
+            z_r.at[t.h],
+            column(other, 0),
+        )
+    kv_gather[0].start()
+
+    half_n = n // 2
+    rising = lax.broadcasted_iota(jnp.int32, (n, 1), 0)
+    query_pos = rising + jnp.where(
+        rising < half_n, order_ref[2 * ctx] * half_n, (order_ref[2 * ctx + 1] - 1) * half_n
+    )
+    lanes = lax.broadcasted_iota(jnp.int32, (1, n), 1)
+    scale = math.log2(math.e) / math.sqrt(HEAD_DIM)
+
+    def attend(w, dy):
+        row = mod4(y + dy)
+        biases = []
+        for i in range(SIDE):
+            c = planes[w] * SIDE * SIDE + row * SIDE + i
+            key_pos = lanes + jnp.where(
+                lanes < half_n, order_ref[2 * c] * half_n, (order_ref[2 * c + 1] - 1) * half_n
+            )
+            biases.append(jnp.where(key_pos <= query_pos, 0.0, -1e30))
+        bias = jnp.concatenate(biases, axis=1)
+        there = pl.ds(pl.multiple_of(row * SIDE * n, SIDE * n), SIDE * n)
+        keys, values = kv[w, 0, there], kv[w, 1, there]
+        for head in range(q_ref.shape[1] // HEAD_DIM):
+            q = q_ref[:, pl.ds(head * HEAD_DIM, HEAD_DIM)]
+            scores = lax.dot_general(q, keys, (((1,), (1,)), ((), ())), preferred_element_type=jnp.float32)
+            scores = scores + bias
+            old = soft_max[head]
+            new = jnp.maximum(old, jnp.max(scores, axis=1, keepdims=True))
+            soft_max[head] = new
+            fade = jnp.exp2((old - new) * scale)
+            probs = jnp.exp2((scores - jnp.concatenate([new] * SIDE, axis=1)) * scale)
+            total = soft_sum[head] * fade
+            for i in range(SIDE):
+                total = total + probs[:, i * n : (i + 1) * n]
+            soft_sum[head] = total
+            soft_acc[head] = soft_acc[head] * fade + jnp.dot(
+                probs.astype(jnp.bfloat16), values, preferred_element_type=jnp.float32
+            )
+
+    kv_gather[0].near()
+    for t in tori:
+        arrived(kv.at[1, t.h, t.rows(0, 0, n)], z_s.at[t.h], z_r.at[t.h])
+    kv_gather[1].start()
+    kv_gather[0].forward(0)
+    kv_gather[0].far()
+    kv_gather[0].forward(1)
+    kv_gather[0].forward(2)
+    kv_gather[1].near()
+    kv_gather[0].forward(3)
+    kv_gather[1].forward(0)
+    kv_gather[1].far()
+    kv_gather[1].forward(1)
+    kv_gather[1].forward(2)
+    kv_gather[0].done()
+    attend(0, 0)
+    kv_gather[1].forward(3)
+    for dy in (-1, 1, 2):
+        attend(0, dy)
+    kv_gather[1].done()
+    for dy in (0, -1, 1, 2):
+        attend(1, dy)
+    for head in range(q_ref.shape[1] // HEAD_DIM):
+        total = jnp.sum(soft_sum[head], axis=1, keepdims=True)
+        att_ref[:, pl.ds(head * HEAD_DIM, HEAD_DIM)] = (soft_acc[head] / total).astype(jnp.bfloat16)
+
     packed = jnp.dot(placing, att_ref[...], preferred_element_type=jnp.float32).astype(jnp.bfloat16)
     pack[...] = packed.reshape(EXPERTS, CAP, CHUNK)
-
-    pl.semaphore_wait(barrier, len(partners))
 
     for w in range(PLANES):
         for d in range(1 - w, EXPERTS):
@@ -157,15 +320,13 @@
             v = xin[w, j].astype(jnp.float32)
             squares += jnp.sum(v * v, axis=1, keepdims=True)
         inverse = lax.rsqrt(squares / WIDTH + 1e-05)
-        logits = jnp.zeros((CAP, EXPERTS), jnp.float32)
+        mine = lax.broadcasted_iota(jnp.int32, (EXPERTS, CHUNK), 0) == e
+        logit = jnp.zeros((CAP, 1), jnp.float32)
         for j in range(EXPERTS):
             cols = pl.ds(j * CHUNK, CHUNK)
             v = xin[w, j].astype(jnp.float32) * inverse * gain_ref[:, cols]
-            logits += jnp.dot(
-                v, router_ref[cols, :], precision=lax.Precision.HIGHEST, preferred_element_type=jnp.float32
-            )
-        mine = lax.broadcasted_iota(jnp.int32, logits.shape, 1) == e
-        logit = jnp.sum(jnp.where(mine, logits, 0.0), axis=1, keepdims=True)
+            weight = jnp.sum(jnp.where(mine, router_ref[:, cols], 0.0), axis=0, keepdims=True)
+            logit += jnp.sum(v * weight, axis=1, keepdims=True)
         gate = 1.0 / (1.0 + jnp.exp(-logit))
         for j in range(EXPERTS):
             cols = pl.ds(j * CHUNK, CHUNK)
@@ -175,56 +336,18 @@
                 g[w, t.h, t.rows(0, 0), cols] = v[t.h * HALF : (t.h + 1) * HALF]
 
     left_half, right_half = pl.ds(0, PIECE_COLS), pl.ds(PIECE_COLS, PIECE_COLS)
-    OFFS = (0, -1, 1, 2)
-
-    def ag_second(w, t, i):
-        piece = g.at[w, t.h, t.rows(OFFS[i], 0)]
-        for s, dq in ((0, 1), (1, -1)):
-            n = 4 + 2 * i + s
-            send(piece, piece, ag_s.at[w, t.h, n], ag_r.at[w, t.h, n], t.dev(0, dq))
-
-    def ag_second_arrived(w, t, i, s):
-        n = 4 + 2 * i + s
-        arrived(g.at[w, t.h, t.rows(OFFS[i], -1 if s == 0 else 1)], ag_s.at[w, t.h, n], ag_r.at[w, t.h, n])
-
-    def ag_start(w):
-        for t in tori:
-            piece = g.at[w, t.h, t.rows(0, 0)]
-            for s, dp in ((0, 1), (1, -1)):
-                send(piece, piece, ag_s.at[w, t.h, s], ag_r.at[w, t.h, s], t.dev(dp, 0))
-        for t in tori:
-            ag_second(w, t, 0)
-
-    def ag_near(w):
-        for t in tori:
-            for s, dp, cols in ((0, -1, left_half), (1, 1, right_half)):
-                arrived(g.at[w, t.h, t.rows(dp, 0)], ag_s.at[w, t.h, s], ag_r.at[w, t.h, s])
-                part_of = g.at[w, t.h, t.rows(dp, 0), cols]
-                send(part_of, part_of, ag_s.at[w, t.h, 2 + s], ag_r.at[w, t.h, 2 + s], t.dev(-dp, 0))
-        for t in tori:
-            ag_second(w, t, 1)
-            ag_second(w, t, 2)
-
-    def ag_far(w):
-        for t in tori:
-            for s, cols in ((0, left_half), (1, right_half)):
-                arrived(g.at[w, t.h, t.rows(2, 0), cols], ag_s.at[w, t.h, 2 + s], ag_r.at[w, t.h, 2 + s])
-            ag_second(w, t, 3)
-
-    OPPOSITE = ((0, 0), (1, 1), (2, 1), (3, 0))
-
-    def ag_forward(w, i):
-        s = OPPOSITE[i][1]
-        dq = 1 if s == 0 else -1
-        for t in tori:
-            ag_second_arrived(w, t, i, s)
-            piece = g.at[w, t.h, t.rows(OFFS[i], -dq)]
-            send(piece, piece, ag_s.at[w, t.h, 12 + i], ag_r.at[w, t.h, 12 + i], t.dev(0, dq))
-
-    def ag_done(w, t):
-        for i in range(4):
-            ag_second_arrived(w, t, i, 1 - OPPOSITE[i][1])
-            arrived(g.at[w, t.h, t.rows(OFFS[i], 2)], ag_s.at[w, t.h, 12 + i], ag_r.at[w, t.h, 12 + i])
+    gather = [
+        Gather(
+            tori,
+            lambda t, dp, dq, w=w: g.at[w, t.h, t.rows(dp, dq)],
+            lambda t, dp, dq, s, w=w: g.at[w, t.h, t.rows(dp, dq), pl.ds(s * PIECE_COLS, PIECE_COLS)],
+            ag_s.at[w],
+            ag_r.at[w],
+            send,
+            arrived,
+        )
+        for w in range(PLANES)
+    ]
 
     def ffn(w, h):
         step = 1280
@@ -341,33 +464,30 @@
             to = lax.rem(e + d, EXPERTS)
             send(fin.at[w, to], ret.at[w, e], back_s.at[w, d], back_r.at[w, d], column(planes[w], d))
 
-    ag = ag_start
     norm(0)
-    ag(0)
+    gather[0].start()
     norm(1)
-    ag_near(0)
-    ag_far(0)
-    ag(1)
-    ag_forward(0, 0)
-    ag_forward(0, 1)
-    ag_near(1)
-    ag_forward(0, 2)
-    ag_forward(0, 3)
-    ag_far(1)
+    gather[0].near()
+    gather[0].far()
+    gather[1].start()
+    gather[0].forward(0)
+    gather[0].forward(1)
+    gather[1].near()
+    gather[0].forward(2)
+    gather[0].forward(3)
+    gather[1].far()
     for load in loads:
         load.wait()
-    ag_done(0, tori[0])
-    ag_done(0, tori[1])
-    ag_forward(1, 0)
-    ag_forward(1, 1)
+    gather[0].done()
+    gather[1].forward(0)
+    gather[1].forward(1)
     ffn(0, 0)
-    ag_forward(1, 2)
-    ag_forward(1, 3)
+    gather[1].forward(2)
+    gather[1].forward(3)
     ffn(0, 1)
     rs_start(0)
     rs_plain(0)
-    ag_done(1, tori[0])
-    ag_done(1, tori[1])
+    gather[1].done()
     for i in range(4):
         rs_joined(0, i)
     ffn(1, 0)
@@ -404,17 +524,24 @@
         copy.wait_send()
 
 
-def moe(attended, routes, norm_gain, router, w_gate, w_up, w_down):
+def per_device(queries, keys, values, block_order, routes, norm_gain, router, w_gate, w_up, w_down):
     vmem = pl.BlockSpec(memory_space=pltpu.VMEM)
+    smem = pl.BlockSpec(memory_space=pltpu.SMEM)
     anywhere = pl.BlockSpec(memory_space=pl.ANY)
     bf16, f32 = jnp.bfloat16, jnp.float32
     dma = pltpu.SemaphoreType.DMA
+    here, features = queries.shape
+    heads = features // HEAD_DIM
     return pl.pallas_call(
-        moe_kernel,
-        out_shape=jax.ShapeDtypeStruct(attended.shape, bf16),
-        in_specs=[vmem, vmem, vmem, vmem, anywhere, anywhere, anywhere],
-        out_specs=vmem,
+        kernel,
+        out_shape=(jax.ShapeDtypeStruct(queries.shape, bf16),) * 2,
+        in_specs=[vmem, vmem, vmem, smem, vmem, vmem, vmem, anywhere, anywhere, anywhere],
+        out_specs=(vmem, vmem),
         scratch_shapes=[
+            pltpu.VMEM((PLANES, 2, SIDE * SIDE * here, HEAD_DIM), bf16),
+            pltpu.VMEM((heads, here, HEAD_DIM), f32),
+            pltpu.VMEM((heads, here, HEAD_DIM), f32),
+            pltpu.VMEM((heads, here, HEAD_DIM), f32),
             pltpu.VMEM((WIDTH, HID), bf16),
             pltpu.VMEM((WIDTH, HID), bf16),
             pltpu.VMEM((HID, WIDTH), bf16),
@@ -431,6 +558,10 @@
             pltpu.VMEM((2, GROUP, HID), f32),
             pltpu.VMEM((GROUP, HID), bf16),
             dma((3,)),
+            dma((2,)),
+            dma((2,)),
+            dma((PLANES, 2, 16)),
+            dma((PLANES, 2, 16)),
             dma((PLANES, EXPERTS)),
             dma((PLANES, EXPERTS)),
             dma((PLANES, 2, 16)),
@@ -443,60 +574,19 @@
         compiler_params=pltpu.CompilerParams(
             collective_id=1, has_side_effects=True, vmem_limit_bytes=62 << 20
         ),
-        name="experts",
+        name="layer",
     )(
-        attended,
+        queries,
+        keys,
+        values,
+        block_order,
         routes.reshape(1, -1),
         norm_gain.reshape(1, -1),
-        router,
+        router.T,
         w_gate[0],
         w_up[0],
         w_down[0],
     )
-
-
-def per_device(queries, keys, values, block_order, routes, norm_gain, router, w_gate, w_up, w_down):
-    rows_here = queries.shape[0]
-    ctx_index = lax.axis_index("ctx")
-    kv_local = keys.shape[1] // HEAD_DIM
-    q_local = queries.shape[1] // HEAD_DIM
-    per_group = q_local // kv_local
-    half_rows = rows_here // 2
-    position = (block_order[:, None] * half_rows + jnp.arange(half_rows, dtype=jnp.int32)[None, :]).reshape(-1)
-    query_pos = lax.dynamic_slice_in_dim(position, ctx_index * rows_here, rows_here)
-    grouped = queries.reshape(rows_here, kv_local, per_group, HEAD_DIM)
-    score_scale = 1.0 / math.sqrt(HEAD_DIM)
-    key_piece = lax.all_gather(keys, "ctx", axis=0, tiled=True)
-    value_piece = lax.all_gather(values, "ctx", axis=0, tiled=True)
-    piece_rows = key_piece.shape[0]
-    scores = (
-        jnp.einsum(
-            "sgqd,rgd->gqsr",
-            grouped,
-            key_piece.reshape(piece_rows, kv_local, HEAD_DIM),
-            preferred_element_type=jnp.float32,
-        )
-        * score_scale
-    )
-    allowed = position[None, :] <= query_pos[:, None]
-    scores = jnp.where(allowed, scores, -1e30)
-    newest_max = jnp.max(scores, axis=3)
-    weights = jnp.where(allowed, jnp.exp(scores - newest_max[..., None]), 0.0)
-    running_sum = jnp.sum(weights, axis=3)
-    weighted = jnp.einsum(
-        "gqsr,rgd->gqsd",
-        weights.astype(jnp.bfloat16),
-        value_piece.reshape(piece_rows, kv_local, HEAD_DIM),
-        preferred_element_type=jnp.float32,
-    )
-    attended = (
-        (weighted / running_sum[..., None])
-        .transpose(2, 0, 1, 3)
-        .reshape(rows_here, q_local * HEAD_DIM)
-    )
-    attended = attended.astype(jnp.bfloat16)
-    routed = moe(attended, routes, norm_gain, router, w_gate, w_up, w_down)
-    return (attended, routed)
 
 
 def solution(mesh):

time: 345 us -> 184 us (0.53)
  waiting for transfers between devices: 152 us -> 0 us
  Pallas kernels: 150 us -> 179 us
  between operations: 14.1 us -> 0.64 us
  matrix products: 9.97 us -> 0 us
  local copies, waits for them, and re-layouts: 12.3 us -> 3.19 us
  other arithmetic: 5.12 us -> 0 us
    all_gather x2 -> x0, waiting for transfers between devices: 151 us -> none  [the longest x1 79 us: per_device(): key_piece = lax.all_gather(keys, 'ctx', axis=0, tiled=True)]
    pallas_call x1, Pallas kernels: 150 us -> 179 us  [per_device(): pl.pallas_call(kernel, out_shape=(jax.ShapeDtypeStruct(queries.shape, bf1...]
    dot_general x2 -> x0, matrix products: 9.97 us -> none  [the longest x1 7.01 us: per_device(): jnp.einsum('gqsr,rgd->gqsd', weights.astype(jnp.bfloat16), value_piece.re...]
    unnamed x7 -> x2, local copies, waits for them, and re-layouts: 12.1 us -> 3.19 us
  transfers between devices with their start and end apart: 2 -> 0, of which waited for: 2 -> 0; matrix products, arithmetic and copies ran while one was open for 4% -> 0% of each run, Pallas kernels for 0% -> 0%
where the time goes in v2:
time: 184 us; the launch traced here: 183 us
  Pallas kernels  179 us (97%)
  local copies, waits for them, and re-layouts  3.19 us (2%)
    pallas_call x1, Pallas kernels, per_device(): pl.pallas_call(kernel, out_shape=(jax.ShapeDtypeStruct(queries.shape, bf1...  179 us

profile of v2, /device:TPU:1, one launch (start us, length us, event | category | flops | bytes accessed | tf_op | source)
XLA Modules:
  0.0 182.9 jit_solution(5121307986448858018)
XLA Ops:
  0.6 179.1 %layer.1 = (bf16[128,640]{1,0:T(8,128)(2,1)}, bf16[128,640]{1,0:T(8,128)(2,1)}) custom-call(bf16[128,640]{1,0:T(8,128)(2,1)} %q_ref.1, bf16[128,128]{1,0:T(8,128)(2,1)} %k_ref.1, bf16[128,128]{1,0:T(8,128)(2,1)} %v_ref.1, s32[64]{0:T(128)} %order_ref.1, s32[1,128]{1,0:T(1,128)} %bitcast.11, f32[1,5120]{1,0:T(1,128)} %bitcast.10, f32[8,5120]{1,0:T(8,128)} %bitcast.9, ...), custom_call_target="tpu_custom_call" | custom-call | tf_op jit(solution)/shard_map/layer/pallas_call | solution.py:535
  179.7 1.6 copy.14
  181.3 1.6 copy.15

commit v3 on v2

v3 whole, which is shorter than its diff:
```python
import functools
import math

import jax
import jax.numpy as jnp
from jax import lax
from jax.experimental import pallas as pl
from jax.experimental.pallas import tpu as pltpu
from jax.sharding import PartitionSpec as P

HEAD_DIM = 128
CAP = 32
MESH = pl.DeviceIdType.MESH

PLANES = 2
SIDE = 4
EXPERTS = 8
WIDTH = 5120
CHUNK = WIDTH // EXPERTS
HALF = CAP // 2
PIECE_COLS = WIDTH // 2
UNIT_COLS = WIDTH // 2
GROUP = SIDE * SIDE * HALF
HID = 256


def mod4(v):
    return lax.rem(v + 2 * SIDE, SIDE)


OFFS = (0, -1, 1, 2)
OPPOSITE = ((0, 0), (1, 1), (2, 1), (3, 0))


class Gather:
    def __init__(self, tori, piece, half, ssem, rsem, send, arrived):
        self.tori, self.piece, self.half = tori, piece, half
        self.ssem, self.rsem, self.send, self.arrived = ssem, rsem, send, arrived

    def sems(self, t, n):
        return self.ssem.at[t.h, n], self.rsem.at[t.h, n]

    def second(self, t, i):
        piece = self.piece(t, OFFS[i], 0)
        for s, dq in ((0, 1), (1, -1)):
            self.send(piece, piece, *self.sems(t, 4 + 2 * i + s), t.dev(0, dq))

    def second_arrived(self, t, i, s):
        self.arrived(self.piece(t, OFFS[i], -1 if s == 0 else 1), *self.sems(t, 4 + 2 * i + s))

    def start(self, t):
        piece = self.piece(t, 0, 0)
        for s, dp in ((0, 1), (1, -1)):
            self.send(piece, piece, *self.sems(t, s), t.dev(dp, 0))
        self.second(t, 0)

    def near(self):
        for t in self.tori:
            for s, dp in ((0, -1), (1, 1)):
                self.arrived(self.piece(t, dp, 0), *self.sems(t, s))
                half = self.half(t, dp, 0, s)
                self.send(half, half, *self.sems(t, 2 + s), t.dev(-dp, 0))
        for t in self.tori:
            self.second(t, 1)
            self.second(t, 2)

    def far(self):
        for t in self.tori:
            for s in range(2):
                self.arrived(self.half(t, 2, 0, s), *self.sems(t, 2 + s))
            self.second(t, 3)

    def forward(self, i):
        s = OPPOSITE[i][1]
        dq = 1 if s == 0 else -1
        for t in self.tori:
            self.second_arrived(t, i, s)
            piece = self.piece(t, OFFS[i], -dq)
            self.send(piece, piece, *self.sems(t, 12 + i), t.dev(0, dq))

    def done(self):
        for t in self.tori:
            for i in range(4):
                self.second_arrived(t, i, 1 - OPPOSITE[i][1])
                self.arrived(self.piece(t, OFFS[i], 2), *self.sems(t, 12 + i))


class Torus:
    def __init__(self, h, plane, y, x, e):
        self.h, self.plane, self.y, self.x, self.e = h, plane, y, x, e

    def at(self, dp, dq):
        if self.h == 0:
            return mod4(self.y + dq), mod4(self.x + dp)
        return mod4(self.y + dp), mod4(self.x + dq)

    def rows(self, dp, dq):
        y, x = self.at(dp, dq)
        return pl.ds(pl.multiple_of((y * SIDE + x) * HALF, HALF), HALF)

    def line(self, dq):
        return mod4((self.y if self.h == 0 else self.x) + dq)

    def along(self, dp):
        return mod4((self.x if self.h == 0 else self.y) + dp)

    def dev(self, dp, dq):
        y, x = self.at(dp, dq)
        return (self.plane * SIDE * SIDE + y * SIDE + x, self.e)


def kernel(
    q_hbm,
    k_hbm,
    v_hbm,
    order_hbm,
    routes_hbm,
    gain_hbm,
    router_hbm,
    wg_hbm,
    wu_hbm,
    wd_hbm,
    att_hbm,
    out_hbm,
    q_ref,
    order_ref,
    routes_ref,
    gain_ref,
    router_ref,
    att_ref,
    out_ref,
    hidden_keys,
    kv,
    soft_max,
    soft_sum,
    soft_acc,
    wg,
    wu,
    wd,
    pack,
    xin,
    g,
    part,
    ru1,
    ru2,
    rv1,
    rv2,
    fin,
    ret,
    acc,
    hid,
    in_sem,
    w_sem,
    z_s,
    z_r,
    kv_s,
    kv_r,
    a2a_s,
    a2a_r,
    ag_s,
    ag_r,
    rs_s,
    rs_r,
    back_s,
    back_r,
):
    ctx = lax.axis_index("ctx")
    e = lax.axis_index("exp")
    plane = ctx // (SIDE * SIDE)
    other = 1 - plane
    spot = lax.rem(ctx, SIDE * SIDE)
    y, x = spot // SIDE, lax.rem(spot, SIDE)
    tori = [Torus(h, plane, y, x, e) for h in range(2)]
    planes = (plane, other)
    sent = []

    def send(src, dst, ssem, rsem, dev):
        copy = pltpu.make_async_remote_copy(
            src_ref=src, dst_ref=dst, send_sem=ssem, recv_sem=rsem, device_id=dev, device_id_type=MESH
        )
        copy.start()
        sent.append(copy)

    def arrived(dst, ssem, rsem):
        pltpu.make_async_remote_copy(
            src_ref=dst, dst_ref=dst, send_sem=ssem, recv_sem=rsem, device_id=tori[0].dev(1, 0), device_id_type=MESH
        ).wait_recv()

    def column(pl_index, d):
        return (pl_index * SIDE * SIDE + spot, lax.rem(e + d, EXPERTS))

    barrier = pltpu.get_barrier_semaphore()
    partners = [column(plane, d) for d in range(1, EXPERTS)]
    partners += [column(other, d) for d in range(EXPERTS)]
    partners += [tori[0].dev(k, 0) for k in (1, -1, 2)] + [tori[0].dev(0, k) for k in (1, -1, 2)]
    for dev in partners:
        pl.semaphore_signal(barrier, inc=1, device_id=dev, device_id_type=MESH)

    inputs = [
        pltpu.make_async_copy(src, dst, in_sem.at[i])
        for i, (src, dst) in enumerate(
            (
                (order_hbm, order_ref),
                (routes_hbm, routes_ref),
                (k_hbm, kv.at[0, 0, tori[0].line(0), tori[0].along(0)]),
                (v_hbm, kv.at[0, 1, tori[1].line(0), tori[1].along(0)]),
                (q_hbm, q_ref),
                (gain_hbm, gain_ref),
                (router_hbm, router_ref),
            )
        )
    ]
    for copy in inputs:
        copy.start()
    loads = [
        pltpu.make_async_copy(wg_hbm, wg, w_sem.at[0]),
        pltpu.make_async_copy(wu_hbm, wu, w_sem.at[1]),
    ]
    for f in range(2):
        for m in range(EXPERTS // 2):
            cols = pl.ds(pl.multiple_of((2 * m + lax.rem(e + f, 2)) * CHUNK, CHUNK), CHUNK)
            loads.append(
                pltpu.make_async_copy(
                    wd_hbm.at[:, cols], wd.at[f, :, pl.ds(m * CHUNK, CHUNK)], w_sem.at[2 + f * 4 + m]
                )
            )
    for load in loads:
        load.start()
    inputs[0].wait()
    inputs[1].wait()

    n = n_rows = att_ref.shape[0]
    onehot = (lax.broadcasted_iota(jnp.int32, (EXPERTS, n_rows), 0) == routes_ref[...]).astype(jnp.float32)
    before = (
        lax.broadcasted_iota(jnp.int32, (n_rows, n_rows), 0)
        < lax.broadcasted_iota(jnp.int32, (n_rows, n_rows), 1)
    ).astype(jnp.bfloat16)
    earlier = jnp.dot(onehot.astype(jnp.bfloat16), before, preferred_element_type=jnp.float32)
    code = jnp.sum(onehot * earlier, axis=0, keepdims=True).astype(jnp.int32) + routes_ref[...] * CAP
    placing = (lax.broadcasted_iota(jnp.int32, (EXPERTS * CAP, n_rows), 0) == code).astype(jnp.bfloat16)


    half_n = n // 2

    def positions(c, shape, dim):
        i = lax.broadcasted_iota(jnp.int32, shape, dim)
        return i + jnp.where(i < half_n, order_ref[2 * c] * half_n, (order_ref[2 * c + 1] - 1) * half_n)

    query_pos = positions(ctx, (1, n), 1)
    for w in range(PLANES):

        @pl.loop(0, SIDE * SIDE)
        def _(i):
            kept = positions(planes[w] * SIDE * SIDE + i, (n, 1), 0) <= query_pos
            rows = pl.ds(pl.multiple_of(i * n, n), n)
            hidden_keys[w, rows, :] = jnp.where(kept, 0.0, -1e30).astype(jnp.bfloat16)

    for copy in inputs[2:]:
        copy.wait()
    pl.semaphore_wait(barrier, len(partners))

    for t in tori:
        piece = (t.h, t.line(0), t.along(0))
        send(kv.at[0, *piece], kv.at[1, *piece], z_s.at[t.h], z_r.at[t.h], column(other, 0))

    def kv_near(w):
        for d in (1, -1, 2):
            for t in tori:
                piece = kv.at[w, t.h, t.line(0), t.along(0)]
                send(piece, piece, kv_s.at[w, t.h, d + 1], kv_r.at[w, t.h, d + 1], t.dev(d, 0))

    def kv_far(w):
        for t in tori:
            for d in (1, -1, 2):
                arrived(kv.at[w, t.h, t.line(0), t.along(-d)], kv_s.at[w, t.h, d + 1], kv_r.at[w, t.h, d + 1])
            line = kv.at[w, t.h, t.line(0)]
            for d in (1, -1, 2):
                send(line, line, kv_s.at[w, t.h, d + 5], kv_r.at[w, t.h, d + 5], t.dev(0, d))

    def kv_done(w):
        for t in tori:
            for d in (1, -1, 2):
                arrived(kv.at[w, t.h, t.line(-d)], kv_s.at[w, t.h, d + 5], kv_r.at[w, t.h, d + 5])

    scale = math.log2(math.e) / math.sqrt(HEAD_DIM)
    heads = q_ref.shape[1] // HEAD_DIM
    each = (
        lax.broadcasted_iota(jnp.int32, (n, n), 0) == lax.broadcasted_iota(jnp.int32, (n, n), 1)
    ).astype(jnp.bfloat16)

    def attend(w):
        everyone = SIDE * SIDE * n
        keys = jnp.concatenate([kv[w, 0].reshape(everyone, HEAD_DIM), hidden_keys[w]], axis=1)
        values = jnp.concatenate(
            [kv[w, 1, i, row] for row in range(SIDE) for i in range(SIDE)], axis=0
        )
        for head in range(heads):
            q = jnp.concatenate([q_ref[:, pl.ds(head * HEAD_DIM, HEAD_DIM)], each], axis=1)
            scores = lax.dot_general(q, keys, (((1,), (1,)), ((), ())), preferred_element_type=jnp.float32)
            new = jnp.max(scores, axis=1, keepdims=True)
            if w > 0:
                old = soft_max[head]
                new = jnp.maximum(old, new)
                fade = jnp.exp2((old - new) * scale)
            probs = jnp.exp2(scores * scale - new * scale)
            total = jnp.sum(probs, axis=1, keepdims=True)
            mixed = jnp.dot(probs.astype(jnp.bfloat16), values, preferred_element_type=jnp.float32)
            if w > 0:
                total = total + soft_sum[head] * fade
                mixed = mixed + soft_acc[head] * fade
                att_ref[:, pl.ds(head * HEAD_DIM, HEAD_DIM)] = (mixed / total).astype(jnp.bfloat16)
            else:
                soft_max[head] = new
                soft_sum[head] = total
                soft_acc[head] = mixed

    kv_near(0)
    kv_far(0)
    for t in tori:
        arrived(kv.at[1, t.h, t.line(0), t.along(0)], z_s.at[t.h], z_r.at[t.h])
    kv_near(1)
    kv_far(1)
    kv_done(0)
    attend(0)
    kv_done(1)
    attend(1)
    attended = pltpu.make_async_copy(att_ref, att_hbm, in_sem.at[7])
    attended.start()

    packed = jnp.dot(placing, att_ref[...], preferred_element_type=jnp.float32).astype(jnp.bfloat16)
    pack[...] = packed.reshape(EXPERTS, CAP, CHUNK)

    def dispatch(w, first, count):
        rows = pl.ds(first, count)
        h = first // HALF
        for d in range(1 - w, EXPERTS):
            to = lax.rem(e + d, EXPERTS)
            send(
                pack.at[to, rows], xin.at[w, e, rows], a2a_s.at[w, h, d], a2a_r.at[w, h, d], column(planes[w], d)
            )

    dispatch(0, 0, HALF)
    dispatch(0, HALF, HALF)
    own = pltpu.make_async_copy(pack.at[e], xin.at[0, e], a2a_s.at[0, 0, 0])
    own.start()

    def norm(w, first, count):
        rows = pl.ds(first, count)
        for d in range(1 - w, EXPERTS):
            src = lax.rem(e - d + EXPERTS, EXPERTS)
            h = first // HALF
            arrived(xin.at[w, src, rows], a2a_s.at[w, h, d], a2a_r.at[w, h, d])
        if w == 0 and first == 0:
            own.wait()
        squares = jnp.zeros((count, 1), jnp.float32)
        for j in range(EXPERTS):
            v = xin[w, j, rows].astype(jnp.float32)
            squares += jnp.sum(v * v, axis=1, keepdims=True)
        inverse = lax.rsqrt(squares / WIDTH + 1e-05)
        mine = lax.broadcasted_iota(jnp.int32, (EXPERTS, CHUNK), 0) == e
        logit = jnp.zeros((count, 1), jnp.float32)
        for j in range(EXPERTS):
            cols = pl.ds(j * CHUNK, CHUNK)
            v = xin[w, j, rows].astype(jnp.float32) * inverse * gain_ref[:, cols]
            weight = jnp.sum(jnp.where(mine, router_ref[:, cols], 0.0), axis=0, keepdims=True)
            logit += jnp.sum(v * weight, axis=1, keepdims=True)
        gate = 1.0 / (1.0 + jnp.exp(-logit))
        for j in range(EXPERTS):
            cols = pl.ds(j * CHUNK, CHUNK)
            v = xin[w, j, rows].astype(jnp.float32) * inverse * gain_ref[:, cols]
            v = (v * gate).astype(jnp.bfloat16)
            for k in range(count // HALF):
                g[w, first // HALF + k, tori[0].rows(0, 0), cols] = v[k * HALF : (k + 1) * HALF]

    left_half, right_half = pl.ds(0, UNIT_COLS // 2), pl.ds(UNIT_COLS // 2, UNIT_COLS // 2)
    gather = [
        Gather(
            tori,
            lambda t, dp, dq, w=w: g.at[w, t.h, t.rows(dp, dq)],
            lambda t, dp, dq, s, w=w: g.at[w, t.h, t.rows(dp, dq), pl.ds(s * PIECE_COLS, PIECE_COLS)],
            ag_s.at[w],
            ag_r.at[w],
            send,
            arrived,
        )
        for w in range(PLANES)
    ]

    def ffn(w, h):
        step = 1280
        acc[...] = jnp.zeros_like(acc)

        @pl.loop(0, WIDTH // step)
        def _(k):
            cols = pl.ds(pl.multiple_of(k * step, step), step)
            rows = g[w, h, :, cols]
            acc[0] += jnp.dot(rows, wg[cols, :], preferred_element_type=jnp.float32)
            acc[1] += jnp.dot(rows, wu[cols, :], preferred_element_type=jnp.float32)

        v = acc[0]
        hid[...] = (v / (1.0 + jnp.exp(-v)) * acc[1]).astype(jnp.bfloat16)
        wide = 512

        @pl.loop(0, UNIT_COLS // wide)
        def _(k):
            cols = pl.ds(pl.multiple_of(k * wide, wide), wide)
            for f in range(2):
                part[w, f, h, :, cols] = jnp.dot(
                    hid[...], wd[f, :, cols], preferred_element_type=jnp.float32
                ).astype(jnp.bfloat16)

    def add(ref, *more):
        total = ref[...].astype(jnp.float32)
        for m in more:
            total = total + m[...].astype(jnp.float32)
        ref[...] = total.astype(jnp.bfloat16)

    mine = pltpu.make_async_copy(fin.at[0, 0, e // 2], ret.at[0, e], back_s.at[0, 0])

    def rs_start(u):
        for t in tori:
            for i, s in OPPOSITE:
                send(
                    part.at[*u, t.h, t.rows(OFFS[i], 2)],
                    ru1.at[*u, t.h, i],
                    rs_s.at[*u, t.h, i],
                    rs_r.at[*u, t.h, i],
                    t.dev(0, 1 if s == 0 else -1),
                )

    def rs_second(u, t, i, s):
        n = 4 + 2 * i + s
        dq = 1 if s == 0 else -1
        send(
            part.at[*u, t.h, t.rows(OFFS[i], dq)],
            ru2.at[*u, t.h, i, s],
            rs_s.at[*u, t.h, n],
            rs_r.at[*u, t.h, n],
            t.dev(0, dq),
        )

    def rs_plain(u):
        for t in tori:
            for i, s in OPPOSITE:
                rs_second(u, t, i, 1 - s)

    def rs_joined(u, i):
        s = OPPOSITE[i][1]
        dq = 1 if s == 0 else -1
        for t in tori:
            arrived(ru1.at[*u, t.h, i], rs_s.at[*u, t.h, i], rs_r.at[*u, t.h, i])
            add(part.at[*u, t.h, t.rows(OFFS[i], dq)], ru1.at[*u, t.h, i])
            rs_second(u, t, i, s)

    def rs_sum(u, t, i):
        for s in range(2):
            n = 4 + 2 * i + s
            arrived(ru2.at[*u, t.h, i, s], rs_s.at[*u, t.h, n], rs_r.at[*u, t.h, n])
        add(part.at[*u, t.h, t.rows(OFFS[i], 0)], ru2.at[*u, t.h, i, 0], ru2.at[*u, t.h, i, 1])

    def rs_turn(u):
        for t in tori:
            rs_sum(u, t, 3)
            for s, dp, cols in ((0, 1, left_half), (1, -1, right_half)):
                send(
                    part.at[*u, t.h, t.rows(2, 0), cols],
                    rv1.at[*u, t.h, s],
                    rs_s.at[*u, t.h, 12 + s],
                    rs_r.at[*u, t.h, 12 + s],
                    t.dev(dp, 0),
                )
        for t in tori:
            for i in (1, 2):
                rs_sum(u, t, i)

    def rs_last(u):
        for t in tori:
            for s, dp, cols in ((0, 1, left_half), (1, -1, right_half)):
                arrived(rv1.at[*u, t.h, s], rs_s.at[*u, t.h, 12 + s], rs_r.at[*u, t.h, 12 + s])
                add(part.at[*u, t.h, t.rows(dp, 0), cols], rv1.at[*u, t.h, s])
                send(
                    part.at[*u, t.h, t.rows(dp, 0)],
                    rv2.at[*u, t.h, s],
                    rs_s.at[*u, t.h, 14 + s],
                    rs_r.at[*u, t.h, 14 + s],
                    t.dev(dp, 0),
                )
        for t in tori:
            rs_sum(u, t, 0)

    def rs_finish(u):
        for t in tori:
            for s in range(2):
                arrived(rv2.at[*u, t.h, s], rs_s.at[*u, t.h, 14 + s], rs_r.at[*u, t.h, 14 + s])
            for m in range(EXPERTS // 2):
                cols = pl.ds(m * CHUNK, CHUNK)
                total = part[*u, t.h, t.rows(0, 0), cols].astype(jnp.float32)
                for s in range(2):
                    total = total + rv2[*u, t.h, s, :, cols].astype(jnp.float32)
                fin[*u, m, pl.ds(t.h * HALF, HALF)] = total.astype(jnp.bfloat16)
        w, f = u
        for d in range(f, EXPERTS, 2):
            to = lax.rem(e + d, EXPERTS)
            if w == 0 and d == 0:
                mine.start()
            else:
                send(fin.at[w, f, to // 2], ret.at[w, e], back_s.at[w, d], back_r.at[w, d], column(planes[w], d))

    for t in tori:
        norm(0, t.h * HALF, HALF)
        gather[0].start(t)
    dispatch(1, 0, CAP)
    gather[0].near()
    gather[0].far()
    gather[0].forward(0)
    gather[0].forward(1)
    norm(1, 0, CAP)
    for t in tori:
        gather[1].start(t)
    gather[0].forward(2)
    gather[0].forward(3)
    gather[1].near()
    gather[1].far()
    for load in loads:
        load.wait()
    gather[0].done()
    gather[1].forward(0)
    gather[1].forward(1)
    ffn(0, 0)
    gather[1].forward(2)
    gather[1].forward(3)
    ffn(0, 1)
    a, b, c, d = (0, 0), (1, 0), (1, 1), (0, 1)

    def rs_begin(u):
        rs_start(u)
        rs_plain(u)

    def rs_join(u):
        for i in range(4):
            rs_joined(u, i)

    rs_begin(a)
    rs_begin(d)
    gather[1].done()
    rs_join(a)
    ffn(1, 0)
    ffn(1, 1)
    rs_begin(b)
    rs_turn(a)
    rs_join(b)
    rs_begin(c)
    rs_last(a)
    rs_turn(b)
    rs_finish(a)
    rs_join(c)
    rs_join(d)
    rs_last(b)
    rs_turn(c)
    rs_finish(b)
    rs_turn(d)
    rs_last(c)
    rs_last(d)
    rs_finish(c)
    rs_finish(d)

    routed = None
    for w in range(PLANES):
        for d in range(1 - w, EXPERTS):
            src = lax.rem(e - d + EXPERTS, EXPERTS)
            arrived(ret.at[w, src], back_s.at[w, d], back_r.at[w, d])
        if w == 0:
            mine.wait()
        rows = ret[w].reshape(EXPERTS * CAP, CHUNK)
        term = lax.dot_general(
            placing, rows, (((0,), (0,)), ((), ())), preferred_element_type=jnp.float32
        )
        routed = term if routed is None else routed + term
    out_ref[...] = routed.astype(jnp.bfloat16)
    result = pltpu.make_async_copy(out_ref, out_hbm, in_sem.at[8])
    result.start()
    attended.wait()
    result.wait()
    for copy in sent:
        copy.wait_send()


def per_device(queries, keys, values, block_order, routes, norm_gain, router, w_gate, w_up, w_down):
    anywhere = pl.BlockSpec(memory_space=pl.ANY)
    bf16, f32 = jnp.bfloat16, jnp.float32
    dma = pltpu.SemaphoreType.DMA
    here, features = queries.shape
    heads = features // HEAD_DIM
    return pl.pallas_call(
        kernel,
        out_shape=(jax.ShapeDtypeStruct(queries.shape, bf16),) * 2,
        in_specs=[anywhere] * 10,
        out_specs=(anywhere, anywhere),
        scratch_shapes=[
            pltpu.VMEM((here, features), bf16),
            pltpu.SMEM(block_order.shape, jnp.int32),
            pltpu.VMEM((1, here), jnp.int32),
            pltpu.VMEM((1, WIDTH), f32),
            pltpu.VMEM((EXPERTS, WIDTH), f32),
            pltpu.VMEM((here, features), bf16),
            pltpu.VMEM((here, features), bf16),
            pltpu.VMEM((PLANES, SIDE * SIDE * here, here), bf16),
            pltpu.VMEM((PLANES, 2, SIDE, SIDE, here, HEAD_DIM), bf16),
            pltpu.VMEM((heads, here, 1), f32),
            pltpu.VMEM((heads, here, 1), f32),
            pltpu.VMEM((heads, here, HEAD_DIM), f32),
            pltpu.VMEM((WIDTH, HID), bf16),
            pltpu.VMEM((WIDTH, HID), bf16),
            pltpu.VMEM((2, HID, UNIT_COLS), bf16),
            pltpu.VMEM((EXPERTS, CAP, CHUNK), bf16),
            pltpu.VMEM((PLANES, EXPERTS, CAP, CHUNK), bf16),
            pltpu.VMEM((PLANES, 2, GROUP, WIDTH), bf16),
            pltpu.VMEM((PLANES, 2, 2, GROUP, UNIT_COLS), bf16),
            pltpu.VMEM((PLANES, 2, 2, 4, HALF, UNIT_COLS), bf16),
            pltpu.VMEM((PLANES, 2, 2, 4, 2, HALF, UNIT_COLS), bf16),
            pltpu.VMEM((PLANES, 2, 2, 2, HALF, UNIT_COLS // 2), bf16),
            pltpu.VMEM((PLANES, 2, 2, 2, HALF, UNIT_COLS), bf16),
            pltpu.VMEM((PLANES, 2, EXPERTS // 2, CAP, CHUNK), bf16),
            pltpu.VMEM((PLANES, EXPERTS, CAP, CHUNK), bf16),
            pltpu.VMEM((2, GROUP, HID), f32),
            pltpu.VMEM((GROUP, HID), bf16),
            dma((9,)),
            dma((10,)),
            dma((2,)),
            dma((2,)),
            dma((PLANES, 2, 8)),
            dma((PLANES, 2, 8)),
            dma((PLANES, 2, EXPERTS)),
            dma((PLANES, 2, EXPERTS)),
            dma((PLANES, 2, 16)),
            dma((PLANES, 2, 16)),
            dma((PLANES, 2, 2, 16)),
            dma((PLANES, 2, 2, 16)),
            dma((PLANES, EXPERTS)),
            dma((PLANES, EXPERTS)),
        ],
        compiler_params=pltpu.CompilerParams(
            collective_id=1, has_side_effects=True, vmem_limit_bytes=62 << 20
        ),
        name="layer",
    )(
        queries,
        keys,
        values,
        block_order,
        routes.reshape(1, -1),
        norm_gain.reshape(1, -1),
        router.T,
        w_gate[0],
        w_up[0],
        w_down[0],
    )


def solution(mesh):
    in_specs = (
        P("ctx", "exp"),
        P("ctx", "exp"),
        P("ctx", "exp"),
        P(),
        P("ctx", None),
        P(),
        P(),
        P("exp", None, "ctx"),
        P("exp", None, "ctx"),
        P("exp", "ctx", None),
    )
    out_specs = (P("ctx", "exp"), P("ctx", "exp"))
    return jax.shard_map(
        per_device, mesh=mesh, in_specs=in_specs, out_specs=out_specs, check_vma=False
    )
```

time: 184 us -> 171 us (0.929)
  Pallas kernels: 179 us -> 167 us
    pallas_call x1, Pallas kernels: 179 us -> 167 us  [per_device(): pl.pallas_call(kernel, out_shape=(jax.ShapeDtypeStruct(queries.shape, bf1...]
where the time goes in v3:
time: 171 us
  Pallas kernels  167 us (98%)
  local copies, waits for them, and re-layouts  3.19 us (2%)
    pallas_call x1, Pallas kernels, per_device(): pl.pallas_call(kernel, out_shape=(jax.ShapeDtypeStruct(queries.shape, bf1...  167 us

profile of v3, /device:TPU:1, one launch (start us, length us, event | category | flops | bytes accessed | tf_op | source)
XLA Modules:
  0.0 170.9 jit_solution(6891255817232713695)
XLA Ops:
  0.6 167.0 %layer.1 = (bf16[128,640]{1,0:T(8,128)(2,1)}, bf16[128,640]{1,0:T(8,128)(2,1)}) custom-call(bf16[128,640]{1,0:T(8,128)(2,1)} %q_hbm.1, bf16[128,128]{1,0:T(8,128)(2,1)} %k_hbm.1, bf16[128,128]{1,0:T(8,128)(2,1)} %v_hbm.1, s32[64]{0:T(128)} %order_hbm.1, s32[1,128]{1,0:T(1,128)} %bitcast.11, f32[1,5120]{1,0:T(1,128)} %bitcast.10, f32[8,5120]{1,0:T(8,128)} %bitcast.9, ...), custom_call_target="tpu_custom_call" | custom-call | tf_op jit(solution)/shard_map/layer/pallas_call | solution.py:594
  167.7 1.6 copy.14
  169.3 1.6 copy.15

commit v4 on v3

--- a/solution.py
+++ b/solution.py
@@ -33,56 +33,46 @@
 
 
 class Gather:
-    def __init__(self, tori, piece, half, ssem, rsem, send, arrived):
-        self.tori, self.piece, self.half = tori, piece, half
+    def __init__(self, tori, piece, half, rows, ssem, rsem, send, arrived):
+        self.tori, self.piece, self.half, self.rows = tori, piece, half, rows
         self.ssem, self.rsem, self.send, self.arrived = ssem, rsem, send, arrived
-
-    def sems(self, t, n):
-        return self.ssem.at[t.h, n], self.rsem.at[t.h, n]
 
     def second(self, t, i):
         piece = self.piece(t, OFFS[i], 0)
         for s, dq in ((0, 1), (1, -1)):
-            self.send(piece, piece, *self.sems(t, 4 + 2 * i + s), t.dev(0, dq))
-
-    def second_arrived(self, t, i, s):
-        self.arrived(self.piece(t, OFFS[i], -1 if s == 0 else 1), *self.sems(t, 4 + 2 * i + s))
+            r = 4 + i if s == OPPOSITE[i][1] else 8
+            self.send(piece, piece, self.ssem.at[2], self.rsem.at[r], t.dev(0, dq))
 
     def start(self, t):
         piece = self.piece(t, 0, 0)
-        for s, dp in ((0, 1), (1, -1)):
-            self.send(piece, piece, *self.sems(t, s), t.dev(dp, 0))
+        for dp in (1, -1):
+            self.send(piece, piece, self.ssem.at[0], self.rsem.at[t.h], t.dev(dp, 0))
         self.second(t, 0)
 
     def near(self):
         for t in self.tori:
+            self.arrived(self.rows(2), self.rsem.at[t.h])
             for s, dp in ((0, -1), (1, 1)):
-                self.arrived(self.piece(t, dp, 0), *self.sems(t, s))
                 half = self.half(t, dp, 0, s)
-                self.send(half, half, *self.sems(t, 2 + s), t.dev(-dp, 0))
+                self.send(half, half, self.ssem.at[1], self.rsem.at[2 + t.h], t.dev(-dp, 0))
         for t in self.tori:
             self.second(t, 1)
             self.second(t, 2)
 
     def far(self):
         for t in self.tori:
-            for s in range(2):
-                self.arrived(self.half(t, 2, 0, s), *self.sems(t, 2 + s))
+            self.arrived(self.rows(1), self.rsem.at[2 + t.h])
             self.second(t, 3)
 
     def forward(self, i):
-        s = OPPOSITE[i][1]
-        dq = 1 if s == 0 else -1
+        dq = 1 if OPPOSITE[i][1] == 0 else -1
+        self.arrived(self.rows(2), self.rsem.at[4 + i])
         for t in self.tori:
-            self.second_arrived(t, i, s)
             piece = self.piece(t, OFFS[i], -dq)
-            self.send(piece, piece, *self.sems(t, 12 + i), t.dev(0, dq))
+            self.send(piece, piece, self.ssem.at[3], self.rsem.at[8], t.dev(0, dq))
 
     def done(self):
-        for t in self.tori:
-            for i in range(4):
-                self.second_arrived(t, i, 1 - OPPOSITE[i][1])
-                self.arrived(self.piece(t, OFFS[i], 2), *self.sems(t, 12 + i))
+        self.arrived(self.rows(16), self.rsem.at[8])
 
 
 class Torus:
@@ -151,8 +141,6 @@
     hid,
     in_sem,
     w_sem,
-    z_s,
-    z_r,
     kv_s,
     kv_r,
     a2a_s,
@@ -172,19 +160,22 @@
     y, x = spot // SIDE, lax.rem(spot, SIDE)
     tori = [Torus(h, plane, y, x, e) for h in range(2)]
     planes = (plane, other)
-    sent = []
 
     def send(src, dst, ssem, rsem, dev):
         copy = pltpu.make_async_remote_copy(
             src_ref=src, dst_ref=dst, send_sem=ssem, recv_sem=rsem, device_id=dev, device_id_type=MESH
         )
         copy.start()
-        sent.append(copy)
-
-    def arrived(dst, ssem, rsem):
+
+    def arrived(ref, rsem):
         pltpu.make_async_remote_copy(
-            src_ref=dst, dst_ref=dst, send_sem=ssem, recv_sem=rsem, device_id=tori[0].dev(1, 0), device_id_type=MESH
+            src_ref=ref, dst_ref=ref, send_sem=rsem, recv_sem=rsem, device_id=tori[0].dev(1, 0), device_id_type=MESH
         ).wait_recv()
+
+    def all_sent(ref, ssem):
+        pltpu.make_async_remote_copy(
+            src_ref=ref, dst_ref=ref, send_sem=ssem, recv_sem=ssem, device_id=tori[0].dev(1, 0), device_id_type=MESH
+        ).wait_send()
 
     def column(pl_index, d):
         return (pl_index * SIDE * SIDE + spot, lax.rem(e + d, EXPERTS))
@@ -221,7 +212,7 @@
             cols = pl.ds(pl.multiple_of((2 * m + lax.rem(e + f, 2)) * CHUNK, CHUNK), CHUNK)
             loads.append(
                 pltpu.make_async_copy(
-                    wd_hbm.at[:, cols], wd.at[f, :, pl.ds(m * CHUNK, CHUNK)], w_sem.at[2 + f * 4 + m]
+                    wd_hbm.at[:, cols], wd.at[f, :, pl.ds(m * CHUNK, CHUNK)], w_sem.at[2]
                 )
             )
     for load in loads:
@@ -261,26 +252,24 @@
 
     for t in tori:
         piece = (t.h, t.line(0), t.along(0))
-        send(kv.at[0, *piece], kv.at[1, *piece], z_s.at[t.h], z_r.at[t.h], column(other, 0))
+        send(kv.at[0, *piece], kv.at[1, *piece], kv_s.at[0], kv_r.at[8], column(other, 0))
 
     def kv_near(w):
         for d in (1, -1, 2):
             for t in tori:
                 piece = kv.at[w, t.h, t.line(0), t.along(0)]
-                send(piece, piece, kv_s.at[w, t.h, d + 1], kv_r.at[w, t.h, d + 1], t.dev(d, 0))
+                send(piece, piece, kv_s.at[1], kv_r.at[4 * w + t.h], t.dev(d, 0))
 
     def kv_far(w):
         for t in tori:
-            for d in (1, -1, 2):
-                arrived(kv.at[w, t.h, t.line(0), t.along(-d)], kv_s.at[w, t.h, d + 1], kv_r.at[w, t.h, d + 1])
+            arrived(kv.at[w, t.h, 0, pl.ds(0, SIDE - 1)], kv_r.at[4 * w + t.h])
             line = kv.at[w, t.h, t.line(0)]
             for d in (1, -1, 2):
-                send(line, line, kv_s.at[w, t.h, d + 5], kv_r.at[w, t.h, d + 5], t.dev(0, d))
+                send(line, line, kv_s.at[2], kv_r.at[4 * w + 2 + t.h], t.dev(0, d))
 
     def kv_done(w):
         for t in tori:
-            for d in (1, -1, 2):
-                arrived(kv.at[w, t.h, t.line(-d)], kv_s.at[w, t.h, d + 5], kv_r.at[w, t.h, d + 5])
+            arrived(kv.at[w, t.h, pl.ds(0, SIDE - 1)], kv_r.at[4 * w + 2 + t.h])
 
     scale = math.log2(math.e) / math.sqrt(HEAD_DIM)
     heads = q_ref.shape[1] // HEAD_DIM
@@ -316,8 +305,7 @@
 
     kv_near(0)
     kv_far(0)
-    for t in tori:
-        arrived(kv.at[1, t.h, t.line(0), t.along(0)], z_s.at[t.h], z_r.at[t.h])
+    arrived(kv.at[1, 0, 0, pl.ds(0, 2)], kv_r.at[8])
     kv_near(1)
     kv_far(1)
     kv_done(0)
@@ -336,20 +324,17 @@
         for d in range(1 - w, EXPERTS):
             to = lax.rem(e + d, EXPERTS)
             send(
-                pack.at[to, rows], xin.at[w, e, rows], a2a_s.at[w, h, d], a2a_r.at[w, h, d], column(planes[w], d)
+                pack.at[to, rows], xin.at[w, e, rows], a2a_s.at[w], a2a_r.at[2 * w + h], column(planes[w], d)
             )
 
     dispatch(0, 0, HALF)
     dispatch(0, HALF, HALF)
-    own = pltpu.make_async_copy(pack.at[e], xin.at[0, e], a2a_s.at[0, 0, 0])
+    own = pltpu.make_async_copy(pack.at[e], xin.at[0, e], in_sem.at[9])
     own.start()
 
     def norm(w, first, count):
         rows = pl.ds(first, count)
-        for d in range(1 - w, EXPERTS):
-            src = lax.rem(e - d + EXPERTS, EXPERTS)
-            h = first // HALF
-            arrived(xin.at[w, src, rows], a2a_s.at[w, h, d], a2a_r.at[w, h, d])
+        arrived(xin.at[w, pl.ds(0, EXPERTS - 1 + w), rows], a2a_r.at[2 * w + first // HALF])
         if w == 0 and first == 0:
             own.wait()
         squares = jnp.zeros((count, 1), jnp.float32)
@@ -378,7 +363,8 @@
             tori,
             lambda t, dp, dq, w=w: g.at[w, t.h, t.rows(dp, dq)],
             lambda t, dp, dq, s, w=w: g.at[w, t.h, t.rows(dp, dq), pl.ds(s * PIECE_COLS, PIECE_COLS)],
-            ag_s.at[w],
+            lambda k, w=w: g.at[w, 0, pl.ds(0, k * HALF)],
+            ag_s,
             ag_r.at[w],
             send,
             arrived,
@@ -415,27 +401,26 @@
             total = total + m[...].astype(jnp.float32)
         ref[...] = total.astype(jnp.bfloat16)
 
-    mine = pltpu.make_async_copy(fin.at[0, 0, e // 2], ret.at[0, e], back_s.at[0, 0])
+    mine = pltpu.make_async_copy(fin.at[0, 0, e // 2], ret.at[0, e], in_sem.at[10])
 
     def rs_start(u):
         for t in tori:
             for i, s in OPPOSITE:
                 send(
                     part.at[*u, t.h, t.rows(OFFS[i], 2)],
-                    ru1.at[*u, t.h, i],
-                    rs_s.at[*u, t.h, i],
-                    rs_r.at[*u, t.h, i],
+                    ru1.at[*u, i, t.h],
+                    rs_s.at[0],
+                    rs_r.at[*u, i],
                     t.dev(0, 1 if s == 0 else -1),
                 )
 
     def rs_second(u, t, i, s):
-        n = 4 + 2 * i + s
         dq = 1 if s == 0 else -1
         send(
             part.at[*u, t.h, t.rows(OFFS[i], dq)],
-            ru2.at[*u, t.h, i, s],
-            rs_s.at[*u, t.h, n],
-            rs_r.at[*u, t.h, n],
+            ru2.at[*u, i, s, t.h],
+            rs_s.at[1],
+            rs_r.at[*u, 4 + i],
             t.dev(0, dq),
         )
 
@@ -447,51 +432,37 @@
     def rs_joined(u, i):
         s = OPPOSITE[i][1]
         dq = 1 if s == 0 else -1
-        for t in tori:
-            arrived(ru1.at[*u, t.h, i], rs_s.at[*u, t.h, i], rs_r.at[*u, t.h, i])
-            add(part.at[*u, t.h, t.rows(OFFS[i], dq)], ru1.at[*u, t.h, i])
+        arrived(ru1.at[*u, i], rs_r.at[*u, i])
+        for t in tori:
+            add(part.at[*u, t.h, t.rows(OFFS[i], dq)], ru1.at[*u, i, t.h])
             rs_second(u, t, i, s)
 
-    def rs_sum(u, t, i):
-        for s in range(2):
-            n = 4 + 2 * i + s
-            arrived(ru2.at[*u, t.h, i, s], rs_s.at[*u, t.h, n], rs_r.at[*u, t.h, n])
-        add(part.at[*u, t.h, t.rows(OFFS[i], 0)], ru2.at[*u, t.h, i, 0], ru2.at[*u, t.h, i, 1])
+    def rs_sum(u, i):
+        arrived(ru2.at[*u, i], rs_r.at[*u, 4 + i])
+        for t in tori:
+            add(part.at[*u, t.h, t.rows(OFFS[i], 0)], ru2.at[*u, i, 0, t.h], ru2.at[*u, i, 1, t.h])
+
+    SIDES = ((0, 1, left_half), (1, -1, right_half))
 
     def rs_turn(u):
-        for t in tori:
-            rs_sum(u, t, 3)
-            for s, dp, cols in ((0, 1, left_half), (1, -1, right_half)):
-                send(
-                    part.at[*u, t.h, t.rows(2, 0), cols],
-                    rv1.at[*u, t.h, s],
-                    rs_s.at[*u, t.h, 12 + s],
-                    rs_r.at[*u, t.h, 12 + s],
-                    t.dev(dp, 0),
-                )
-        for t in tori:
-            for i in (1, 2):
-                rs_sum(u, t, i)
+        rs_sum(u, 3)
+        for t in tori:
+            for s, dp, cols in SIDES:
+                send(part.at[*u, t.h, t.rows(2, 0), cols], rv1.at[*u, t.h, s], rs_s.at[2], rs_r.at[*u, 8], t.dev(dp, 0))
+        rs_sum(u, 1)
+        rs_sum(u, 2)
 
     def rs_last(u):
-        for t in tori:
-            for s, dp, cols in ((0, 1, left_half), (1, -1, right_half)):
-                arrived(rv1.at[*u, t.h, s], rs_s.at[*u, t.h, 12 + s], rs_r.at[*u, t.h, 12 + s])
+        arrived(rv1.at[*u], rs_r.at[*u, 8])
+        for t in tori:
+            for s, dp, cols in SIDES:
                 add(part.at[*u, t.h, t.rows(dp, 0), cols], rv1.at[*u, t.h, s])
-                send(
-                    part.at[*u, t.h, t.rows(dp, 0)],
-                    rv2.at[*u, t.h, s],
-                    rs_s.at[*u, t.h, 14 + s],
-                    rs_r.at[*u, t.h, 14 + s],
-                    t.dev(dp, 0),
-                )
-        for t in tori:
-            rs_sum(u, t, 0)
+                send(part.at[*u, t.h, t.rows(dp, 0)], rv2.at[*u, t.h, s], rs_s.at[3], rs_r.at[*u, 9], t.dev(dp, 0))
+        rs_sum(u, 0)
 
     def rs_finish(u):
-        for t in tori:
-            for s in range(2):
-                arrived(rv2.at[*u, t.h, s], rs_s.at[*u, t.h, 14 + s], rs_r.at[*u, t.h, 14 + s])
+        arrived(rv2.at[*u], rs_r.at[*u, 9])
+        for t in tori:
             for m in range(EXPERTS // 2):
                 cols = pl.ds(m * CHUNK, CHUNK)
                 total = part[*u, t.h, t.rows(0, 0), cols].astype(jnp.float32)
@@ -504,7 +475,7 @@
             if w == 0 and d == 0:
                 mine.start()
             else:
-                send(fin.at[w, f, to // 2], ret.at[w, e], back_s.at[w, d], back_r.at[w, d], column(planes[w], d))
+                send(fin.at[w, f, to // 2], ret.at[w, e], back_s.at[w], back_r.at[w], column(planes[w], d))
 
     for t in tori:
         norm(0, t.h * HALF, HALF)
@@ -521,8 +492,9 @@
     gather[0].forward(3)
     gather[1].near()
     gather[1].far()
-    for load in loads:
-        load.wait()
+    loads[0].wait()
+    loads[1].wait()
+    pltpu.make_async_copy(wd, wd, w_sem.at[2]).wait()
     gather[0].done()
     gather[1].forward(0)
     gather[1].forward(1)
@@ -566,9 +538,7 @@
 
     routed = None
     for w in range(PLANES):
-        for d in range(1 - w, EXPERTS):
-            src = lax.rem(e - d + EXPERTS, EXPERTS)
-            arrived(ret.at[w, src], back_s.at[w, d], back_r.at[w, d])
+        arrived(ret.at[w, pl.ds(0, EXPERTS - 1 + w)], back_r.at[w])
         if w == 0:
             mine.wait()
         rows = ret[w].reshape(EXPERTS * CAP, CHUNK)
@@ -581,8 +551,19 @@
     result.start()
     attended.wait()
     result.wait()
-    for copy in sent:
-        copy.wait_send()
+    all_sent(kv.at[0, 0, 0, pl.ds(0, 2)], kv_s.at[0])
+    all_sent(kv.at[0, 0, pl.ds(0, SIDE - 1)], kv_s.at[1])
+    all_sent(kv.at[:, :, pl.ds(0, SIDE - 1)], kv_s.at[2])
+    all_sent(xin.at[0, pl.ds(0, EXPERTS - 1)], a2a_s.at[0])
+    all_sent(xin.at[1], a2a_s.at[1])
+    all_sent(g.at[0, 0, pl.ds(0, 8 * HALF)], ag_s.at[0])
+    all_sent(g.at[0, 0, pl.ds(0, 4 * HALF)], ag_s.at[1])
+    all_sent(g.at[0], ag_s.at[2])
+    all_sent(g.at[0, 0], ag_s.at[3])
+    for i, ref in enumerate((ru1, ru2, rv1, rv2)):
+        all_sent(ref, rs_s.at[i])
+    all_sent(ret.at[0, pl.ds(0, EXPERTS - 1)], back_s.at[0])
+    all_sent(ret.at[1], back_s.at[1])
 
 
 def per_device(queries, keys, values, block_order, routes, norm_gain, router, w_gate, w_up, w_down):
@@ -616,28 +597,26 @@
             pltpu.VMEM((PLANES, EXPERTS, CAP, CHUNK), bf16),
             pltpu.VMEM((PLANES, 2, GROUP, WIDTH), bf16),
             pltpu.VMEM((PLANES, 2, 2, GROUP, UNIT_COLS), bf16),
-            pltpu.VMEM((PLANES, 2, 2, 4, HALF, UNIT_COLS), bf16),
-            pltpu.VMEM((PLANES, 2, 2, 4, 2, HALF, UNIT_COLS), bf16),
+            pltpu.VMEM((PLANES, 2, 4, 2, HALF, UNIT_COLS), bf16),
+            pltpu.VMEM((PLANES, 2, 4, 2, 2, HALF, UNIT_COLS), bf16),
             pltpu.VMEM((PLANES, 2, 2, 2, HALF, UNIT_COLS // 2), bf16),
             pltpu.VMEM((PLANES, 2, 2, 2, HALF, UNIT_COLS), bf16),
             pltpu.VMEM((PLANES, 2, EXPERTS // 2, CAP, CHUNK), bf16),
             pltpu.VMEM((PLANES, EXPERTS, CAP, CHUNK), bf16),
             pltpu.VMEM((2, GROUP, HID), f32),
             pltpu.VMEM((GROUP, HID), bf16),
+            dma((11,)),
+            dma((3,)),
+            dma((3,)),
             dma((9,)),
-            dma((10,)),
+            dma((2,)),
+            dma((3,)),
+            dma((4,)),
+            dma((PLANES, 9)),
+            dma((4,)),
+            dma((PLANES, 2, 10)),
             dma((2,)),
             dma((2,)),
-            dma((PLANES, 2, 8)),
-            dma((PLANES, 2, 8)),
-            dma((PLANES, 2, EXPERTS)),
-            dma((PLANES, 2, EXPERTS)),
-            dma((PLANES, 2, 16)),
-            dma((PLANES, 2, 16)),
-            dma((PLANES, 2, 2, 16)),
-            dma((PLANES, 2, 2, 16)),
-            dma((PLANES, EXPERTS)),
-            dma((PLANES, EXPERTS)),
         ],
         compiler_params=pltpu.CompilerParams(
             collective_id=1, has_side_effects=True, vmem_limit_bytes=62 << 20

time: 171 us -> 168 us (0.982)
  Pallas kernels: 167 us -> 164 us
    pallas_call x1, Pallas kernels: 167 us -> 164 us  [per_device(): pl.pallas_call(kernel, out_shape=(jax.ShapeDtypeStruct(queries.shape, bf1...]
where the time goes in v4:
time: 168 us
  Pallas kernels  164 us (98%)
  local copies, waits for them, and re-layouts  3.19 us (2%)
    pallas_call x1, Pallas kernels, per_device(): pl.pallas_call(kernel, out_shape=(jax.ShapeDtypeStruct(queries.shape, bf1...  164 us

profile of v4, /device:TPU:1, one launch (start us, length us, event | category | flops | bytes accessed | tf_op | source)
XLA Modules:
  0.0 168.2 jit_solution(16039887780896718143)
XLA Ops:
  0.6 164.3 %layer.1 = (bf16[128,640]{1,0:T(8,128)(2,1)}, bf16[128,640]{1,0:T(8,128)(2,1)}) custom-call(bf16[128,640]{1,0:T(8,128)(2,1)} %q_hbm.1, bf16[128,128]{1,0:T(8,128)(2,1)} %k_hbm.1, bf16[128,128]{1,0:T(8,128)(2,1)} %v_hbm.1, s32[64]{0:T(128)} %order_hbm.1, s32[1,128]{1,0:T(1,128)} %bitcast.11, f32[1,5120]{1,0:T(1,128)} %bitcast.10, f32[8,5120]{1,0:T(8,128)} %bitcast.9, ...), custom_call_target="tpu_custom_call" | custom-call | tf_op jit(solution)/shard_map/layer/pallas_call | solution.py:575
  165.0 1.6 copy.14
  166.6 1.6 copy.15

commit v5 on v4

--- a/solution.py
+++ b/solution.py
@@ -110,8 +110,7 @@
     wg_hbm,
     wu_hbm,
     wd_hbm,
-    att_hbm,
-    out_hbm,
+    both_hbm,
     q_ref,
     order_ref,
     routes_ref,
@@ -312,7 +311,7 @@
     attend(0)
     kv_done(1)
     attend(1)
-    attended = pltpu.make_async_copy(att_ref, att_hbm, in_sem.at[7])
+    attended = pltpu.make_async_copy(att_ref, both_hbm.at[0], in_sem.at[7])
     attended.start()
 
     packed = jnp.dot(placing, att_ref[...], preferred_element_type=jnp.float32).astype(jnp.bfloat16)
@@ -526,14 +525,14 @@
     rs_turn(b)
     rs_finish(a)
     rs_join(c)
-    rs_join(d)
     rs_last(b)
     rs_turn(c)
+    rs_join(d)
     rs_finish(b)
+    rs_last(c)
     rs_turn(d)
-    rs_last(c)
+    rs_finish(c)
     rs_last(d)
-    rs_finish(c)
     rs_finish(d)
 
     routed = None
@@ -547,7 +546,7 @@
         )
         routed = term if routed is None else routed + term
     out_ref[...] = routed.astype(jnp.bfloat16)
-    result = pltpu.make_async_copy(out_ref, out_hbm, in_sem.at[8])
+    result = pltpu.make_async_copy(out_ref, both_hbm.at[1], in_sem.at[8])
     result.start()
     attended.wait()
     result.wait()
@@ -572,11 +571,11 @@
     dma = pltpu.SemaphoreType.DMA
     here, features = queries.shape
     heads = features // HEAD_DIM
-    return pl.pallas_call(
+    both = pl.pallas_call(
         kernel,
-        out_shape=(jax.ShapeDtypeStruct(queries.shape, bf16),) * 2,
+        out_shape=jax.ShapeDtypeStruct((2, *queries.shape), bf16),
         in_specs=[anywhere] * 10,
-        out_specs=(anywhere, anywhere),
+        out_specs=anywhere,
         scratch_shapes=[
             pltpu.VMEM((here, features), bf16),
             pltpu.SMEM(block_order.shape, jnp.int32),
@@ -634,6 +633,7 @@
         w_up[0],
         w_down[0],
     )
+    return both[0], both[1]
 
 
 def solution(mesh):

time: 168 us -> 167 us (level)
    unnamed x2 -> x0, local copies, waits for them, and re-layouts: 3.19 us -> none
    squeeze x0 -> x1, local copies, waits for them, and re-layouts: none -> 1.75 us  [per_device(): return (both[0], both[1])]
where the time goes in v5:
time: 167 us
  Pallas kernels  165 us (99%)
  local copies, waits for them, and re-layouts  1.75 us (1%)
    pallas_call x1, Pallas kernels, per_device(): pl.pallas_call(kernel, out_shape=jax.ShapeDtypeStruct((2, *queries.shape)...  165 us

profile of v5, /device:TPU:1, one launch (start us, length us, event | category | flops | bytes accessed | tf_op | source)
XLA Modules:
  0.0 166.9 jit_solution(12880734151677321220)
XLA Ops:
  0.6 164.5 %layer.1 = bf16[2,128,640]{2,1,0:T(8,128)(2,1)} custom-call(bf16[128,640]{1,0:T(8,128)(2,1)} %q_hbm.1, bf16[128,128]{1,0:T(8,128)(2,1)} %k_hbm.1, bf16[128,128]{1,0:T(8,128)(2,1)} %v_hbm.1, s32[64]{0:T(128)} %order_hbm.1, s32[1,128]{1,0:T(1,128)} %bitcast.15, f32[1,5120]{1,0:T(1,128)} %bitcast.14, f32[8,5120]{1,0:T(8,128)} %bitcast.13, ...), custom_call_target="tpu_custom_call" | custom-call | tf_op jit(solution)/shard_map/layer/pallas_call | solution.py:574
  165.2 1.7 %slice_bitcast_fusion = (bf16[128,640]{1,0:T(8,128)(2,1)}, bf16[128,640]{1,0:T(8,128)(2,1)}) fusion(bf16[2,128,640]{2,1,0:T(8,128)(2,1)} %layer.1), kind=kLoop, calls=%fused_computation | loop fusion | bytes 655360 | tf_op jit(solution)/shard_map/squeeze | solution.py:636

commit v6 on v5

--- a/solution.py
+++ b/solution.py
@@ -206,13 +206,16 @@
         pltpu.make_async_copy(wg_hbm, wg, w_sem.at[0]),
         pltpu.make_async_copy(wu_hbm, wu, w_sem.at[1]),
     ]
+    distances = ((1, 2), (3, 0))
+
+    def receiver(f, k):
+        return lax.rem(e // 2 + distances[f][k // 2], EXPERTS // 2) * 2 + lax.rem(e + k, 2)
+
     for f in range(2):
-        for m in range(EXPERTS // 2):
-            cols = pl.ds(pl.multiple_of((2 * m + lax.rem(e + f, 2)) * CHUNK, CHUNK), CHUNK)
+        for k in range(EXPERTS // 2):
+            cols = pl.ds(pl.multiple_of(receiver(f, k) * CHUNK, CHUNK), CHUNK)
             loads.append(
-                pltpu.make_async_copy(
-                    wd_hbm.at[:, cols], wd.at[f, :, pl.ds(m * CHUNK, CHUNK)], w_sem.at[2]
-                )
+                pltpu.make_async_copy(wd_hbm.at[:, cols], wd.at[f, :, pl.ds(k * CHUNK, CHUNK)], w_sem.at[2])
             )
     for load in loads:
         load.start()
@@ -242,8 +245,7 @@
         @pl.loop(0, SIDE * SIDE)
         def _(i):
             kept = positions(planes[w] * SIDE * SIDE + i, (n, 1), 0) <= query_pos
-            rows = pl.ds(pl.multiple_of(i * n, n), n)
-            hidden_keys[w, rows, :] = jnp.where(kept, 0.0, -1e30).astype(jnp.bfloat16)
+            hidden_keys[w, i] = jnp.where(kept, 0.0, -1e30).astype(jnp.bfloat16)
 
     for copy in inputs[2:]:
         copy.wait()
@@ -263,12 +265,19 @@
         for t in tori:
             arrived(kv.at[w, t.h, 0, pl.ds(0, SIDE - 1)], kv_r.at[4 * w + t.h])
             line = kv.at[w, t.h, t.line(0)]
-            for d in (1, -1, 2):
+            for d in (1, -1):
                 send(line, line, kv_s.at[2], kv_r.at[4 * w + 2 + t.h], t.dev(0, d))
 
+    def kv_forward(w):
+        for t in tori:
+            arrived(kv.at[w, t.h, pl.ds(0, 2)], kv_r.at[4 * w + 2 + t.h])
+            for s, d in ((0, 1), (1, -1)):
+                half = kv.at[w, t.h, t.line(-d), pl.ds(2 * s, 2)]
+                send(half, half, kv_s.at[3], kv_r.at[9 + 2 * w + t.h], t.dev(0, d))
+
     def kv_done(w):
         for t in tori:
-            arrived(kv.at[w, t.h, pl.ds(0, SIDE - 1)], kv_r.at[4 * w + 2 + t.h])
+            arrived(kv.at[w, t.h, 0], kv_r.at[9 + 2 * w + t.h])
 
     scale = math.log2(math.e) / math.sqrt(HEAD_DIM)
     heads = q_ref.shape[1] // HEAD_DIM
@@ -276,41 +285,51 @@
         lax.broadcasted_iota(jnp.int32, (n, n), 0) == lax.broadcasted_iota(jnp.int32, (n, n), 1)
     ).astype(jnp.bfloat16)
 
-    def attend(w):
-        everyone = SIDE * SIDE * n
-        keys = jnp.concatenate([kv[w, 0].reshape(everyone, HEAD_DIM), hidden_keys[w]], axis=1)
-        values = jnp.concatenate(
-            [kv[w, 1, i, row] for row in range(SIDE) for i in range(SIDE)], axis=0
-        )
+    def attend(w, blocks, first=False, last=False):
+        places = [(mod4(y + dy), mod4(x + dx)) for dy, dx in blocks]
+        keys = jnp.concatenate([kv[w, 0, r, i] for r, i in places], axis=0)
+        values = jnp.concatenate([kv[w, 1, i, r] for r, i in places], axis=0)
+        hide = jnp.concatenate([hidden_keys[w, r * SIDE + i] for r, i in places], axis=0)
+        keys = jnp.concatenate([keys, hide], axis=1)
         for head in range(heads):
             q = jnp.concatenate([q_ref[:, pl.ds(head * HEAD_DIM, HEAD_DIM)], each], axis=1)
             scores = lax.dot_general(q, keys, (((1,), (1,)), ((), ())), preferred_element_type=jnp.float32)
             new = jnp.max(scores, axis=1, keepdims=True)
-            if w > 0:
+            if not first:
                 old = soft_max[head]
                 new = jnp.maximum(old, new)
                 fade = jnp.exp2((old - new) * scale)
             probs = jnp.exp2(scores * scale - new * scale)
             total = jnp.sum(probs, axis=1, keepdims=True)
             mixed = jnp.dot(probs.astype(jnp.bfloat16), values, preferred_element_type=jnp.float32)
-            if w > 0:
+            if not first:
                 total = total + soft_sum[head] * fade
                 mixed = mixed + soft_acc[head] * fade
+            if last:
                 att_ref[:, pl.ds(head * HEAD_DIM, HEAD_DIM)] = (mixed / total).astype(jnp.bfloat16)
             else:
                 soft_max[head] = new
                 soft_sum[head] = total
                 soft_acc[head] = mixed
 
+    everyone = [(dy, dx) for dy in range(SIDE) for dx in range(SIDE)]
+    close = [(dy, dx) for dy, dx in everyone if dy != 2 and dx != 2]
+    distant = [block for block in everyone if block not in close]
+
     kv_near(0)
     kv_far(0)
     arrived(kv.at[1, 0, 0, pl.ds(0, 2)], kv_r.at[8])
     kv_near(1)
+    kv_forward(0)
+    attend(0, close, first=True)
     kv_far(1)
     kv_done(0)
-    attend(0)
+    attend(0, distant)
+    kv_forward(1)
+    attend(1, close)
     kv_done(1)
-    attend(1)
+    attend(1, distant, last=True)
+
     attended = pltpu.make_async_copy(att_ref, both_hbm.at[0], in_sem.at[7])
     attended.start()
 
@@ -356,7 +375,7 @@
             for k in range(count // HALF):
                 g[w, first // HALF + k, tori[0].rows(0, 0), cols] = v[k * HALF : (k + 1) * HALF]
 
-    left_half, right_half = pl.ds(0, UNIT_COLS // 2), pl.ds(UNIT_COLS // 2, UNIT_COLS // 2)
+
     gather = [
         Gather(
             tori,
@@ -402,79 +421,97 @@
 
     mine = pltpu.make_async_copy(fin.at[0, 0, e // 2], ret.at[0, e], in_sem.at[10])
 
-    def rs_start(u):
+    class Unit:
+        def __init__(self, n, w, f, chunks):
+            self.n, self.w, self.f, self.chunks = n, w, f, chunks
+            self.first, self.count = chunks[0] * CHUNK, len(chunks) * CHUNK
+            self.cols = pl.ds(self.first, self.count)
+
+        def part(self, t, dp, dq):
+            return part.at[self.w, self.f, t.h, t.rows(dp, dq), self.cols]
+
+        def half_part(self, t, dp, s):
+            half = self.count // 2
+            return part.at[self.w, self.f, t.h, t.rows(dp, 0), pl.ds(self.first + s * half, half)]
+
+        def via(self, i, h):
+            return ru1.at[self.w, self.f, i, h, :, self.cols]
+
+        def second(self, i, s, h):
+            return ru2.at[self.w, self.f, i, s, h, :, self.cols]
+
+        def half_via(self, h, s):
+            return rv1.at[self.w, self.f, h, s, :, pl.ds(self.first // 2, self.count // 2)]
+
+        def first_axis(self, h, s):
+            return rv2.at[self.w, self.f, h, s, :, self.cols]
+
+        def sem(self, k):
+            return rs_r.at[self.n, k]
+
+    both = slice(None)
+
+    def rs_begin(u):
         for t in tori:
             for i, s in OPPOSITE:
-                send(
-                    part.at[*u, t.h, t.rows(OFFS[i], 2)],
-                    ru1.at[*u, i, t.h],
-                    rs_s.at[0],
-                    rs_r.at[*u, i],
-                    t.dev(0, 1 if s == 0 else -1),
-                )
+                send(u.part(t, OFFS[i], 2), u.via(i, t.h), rs_s.at[0], u.sem(i), t.dev(0, 1 if s == 0 else -1))
+        for t in tori:
+            for i, s in OPPOSITE:
+                rs_second(u, t, i, 1 - s)
 
     def rs_second(u, t, i, s):
         dq = 1 if s == 0 else -1
-        send(
-            part.at[*u, t.h, t.rows(OFFS[i], dq)],
-            ru2.at[*u, i, s, t.h],
-            rs_s.at[1],
-            rs_r.at[*u, 4 + i],
-            t.dev(0, dq),
-        )
-
-    def rs_plain(u):
-        for t in tori:
-            for i, s in OPPOSITE:
-                rs_second(u, t, i, 1 - s)
-
-    def rs_joined(u, i):
-        s = OPPOSITE[i][1]
-        dq = 1 if s == 0 else -1
-        arrived(ru1.at[*u, i], rs_r.at[*u, i])
-        for t in tori:
-            add(part.at[*u, t.h, t.rows(OFFS[i], dq)], ru1.at[*u, i, t.h])
-            rs_second(u, t, i, s)
+        send(u.part(t, OFFS[i], dq), u.second(i, s, t.h), rs_s.at[1], u.sem(4 + i), t.dev(0, dq))
+
+    def rs_join(u):
+        for i, s in OPPOSITE:
+            arrived(u.via(i, both), u.sem(i))
+            for t in tori:
+                add(u.part(t, OFFS[i], 1 if s == 0 else -1), u.via(i, t.h))
+                rs_second(u, t, i, s)
 
     def rs_sum(u, i):
-        arrived(ru2.at[*u, i], rs_r.at[*u, 4 + i])
-        for t in tori:
-            add(part.at[*u, t.h, t.rows(OFFS[i], 0)], ru2.at[*u, i, 0, t.h], ru2.at[*u, i, 1, t.h])
-
-    SIDES = ((0, 1, left_half), (1, -1, right_half))
+        arrived(u.second(i, both, both), u.sem(4 + i))
+        for t in tori:
+            add(u.part(t, OFFS[i], 0), u.second(i, 0, t.h), u.second(i, 1, t.h))
 
     def rs_turn(u):
         rs_sum(u, 3)
         for t in tori:
-            for s, dp, cols in SIDES:
-                send(part.at[*u, t.h, t.rows(2, 0), cols], rv1.at[*u, t.h, s], rs_s.at[2], rs_r.at[*u, 8], t.dev(dp, 0))
+            for s, dp in ((0, 1), (1, -1)):
+                send(u.half_part(t, 2, s), u.half_via(t.h, s), rs_s.at[2], u.sem(8), t.dev(dp, 0))
         rs_sum(u, 1)
         rs_sum(u, 2)
 
     def rs_last(u):
-        arrived(rv1.at[*u], rs_r.at[*u, 8])
-        for t in tori:
-            for s, dp, cols in SIDES:
-                add(part.at[*u, t.h, t.rows(dp, 0), cols], rv1.at[*u, t.h, s])
-                send(part.at[*u, t.h, t.rows(dp, 0)], rv2.at[*u, t.h, s], rs_s.at[3], rs_r.at[*u, 9], t.dev(dp, 0))
+        arrived(u.half_via(both, both), u.sem(8))
+        for t in tori:
+            for s, dp in ((0, 1), (1, -1)):
+                add(u.half_part(t, dp, s), u.half_via(t.h, s))
+                send(u.part(t, dp, 0), u.first_axis(t.h, s), rs_s.at[3], u.sem(9), t.dev(dp, 0))
         rs_sum(u, 0)
 
+    mine = pltpu.make_async_copy(fin.at[0, 1, 2], ret.at[0, e], in_sem.at[10])
+
     def rs_finish(u):
-        arrived(rv2.at[*u], rs_r.at[*u, 9])
-        for t in tori:
-            for m in range(EXPERTS // 2):
-                cols = pl.ds(m * CHUNK, CHUNK)
-                total = part[*u, t.h, t.rows(0, 0), cols].astype(jnp.float32)
+        arrived(u.first_axis(both, both), u.sem(9))
+        w, f = u.w, u.f
+        for k in u.chunks:
+            cols = pl.ds(k * CHUNK, CHUNK)
+            for t in tori:
+                total = part[w, f, t.h, t.rows(0, 0), cols].astype(jnp.float32)
                 for s in range(2):
-                    total = total + rv2[*u, t.h, s, :, cols].astype(jnp.float32)
-                fin[*u, m, pl.ds(t.h * HALF, HALF)] = total.astype(jnp.bfloat16)
-        w, f = u
-        for d in range(f, EXPERTS, 2):
-            to = lax.rem(e + d, EXPERTS)
-            if w == 0 and d == 0:
+                    total = total + rv2[w, f, t.h, s, :, cols].astype(jnp.float32)
+                fin[w, f, k, pl.ds(t.h * HALF, HALF)] = total.astype(jnp.bfloat16)
+            if (w, f, k) == (0, 1, 2):
                 mine.start()
             else:
-                send(fin.at[w, f, to // 2], ret.at[w, e], back_s.at[w], back_r.at[w], column(planes[w], d))
+                to = receiver(f, k)
+                dev = (planes[w] * SIDE * SIDE + spot, to)
+                send(fin.at[w, f, k], ret.at[w, e], back_s.at[w], back_r.at[w], dev)
+
+    a, b, c = Unit(0, 0, 0, range(4)), Unit(1, 1, 0, range(4)), Unit(2, 1, 1, range(4))
+    p, q = Unit(3, 0, 1, range(2)), Unit(4, 0, 1, range(2, 4))
 
     for t in tori:
         norm(0, t.h * HALF, HALF)
@@ -501,18 +538,8 @@
     gather[1].forward(2)
     gather[1].forward(3)
     ffn(0, 1)
-    a, b, c, d = (0, 0), (1, 0), (1, 1), (0, 1)
-
-    def rs_begin(u):
-        rs_start(u)
-        rs_plain(u)
-
-    def rs_join(u):
-        for i in range(4):
-            rs_joined(u, i)
-
     rs_begin(a)
-    rs_begin(d)
+    rs_begin(p)
     gather[1].done()
     rs_join(a)
     ffn(1, 0)
@@ -525,15 +552,20 @@
     rs_turn(b)
     rs_finish(a)
     rs_join(c)
+    rs_join(p)
+    rs_begin(q)
     rs_last(b)
     rs_turn(c)
-    rs_join(d)
     rs_finish(b)
+    rs_turn(p)
     rs_last(c)
-    rs_turn(d)
+    rs_join(q)
+    rs_last(p)
     rs_finish(c)
-    rs_last(d)
-    rs_finish(d)
+    rs_turn(q)
+    rs_finish(p)
+    rs_last(q)
+    rs_finish(q)
 
     routed = None
     for w in range(PLANES):
@@ -552,7 +584,8 @@
     result.wait()
     all_sent(kv.at[0, 0, 0, pl.ds(0, 2)], kv_s.at[0])
     all_sent(kv.at[0, 0, pl.ds(0, SIDE - 1)], kv_s.at[1])
-    all_sent(kv.at[:, :, pl.ds(0, SIDE - 1)], kv_s.at[2])
+    all_sent(kv.at[:, :, pl.ds(0, 2)], kv_s.at[2])
+    all_sent(kv.at[:, :, 0], kv_s.at[3])
     all_sent(xin.at[0, pl.ds(0, EXPERTS - 1)], a2a_s.at[0])
     all_sent(xin.at[1], a2a_s.at[1])
     all_sent(g.at[0, 0, pl.ds(0, 8 * HALF)], ag_s.at[0])
@@ -584,7 +617,7 @@
             pltpu.VMEM((EXPERTS, WIDTH), f32),
             pltpu.VMEM((here, features), bf16),
             pltpu.VMEM((here, features), bf16),
-            pltpu.VMEM((PLANES, SIDE * SIDE * here, here), bf16),
+            pltpu.VMEM((PLANES, SIDE * SIDE, here, here), bf16),
             pltpu.VMEM((PLANES, 2, SIDE, SIDE, here, HEAD_DIM), bf16),
             pltpu.VMEM((heads, here, 1), f32),
             pltpu.VMEM((heads, here, 1), f32),
@@ -606,14 +639,14 @@
             pltpu.VMEM((GROUP, HID), bf16),
             dma((11,)),
             dma((3,)),
-            dma((3,)),
-            dma((9,)),
+            dma((4,)),
+            dma((13,)),
             dma((2,)),
             dma((3,)),
             dma((4,)),
             dma((PLANES, 9)),
             dma((4,)),
-            dma((PLANES, 2, 10)),
+            dma((5, 10)),
             dma((2,)),
             dma((2,)),
         ],

time: 167 us -> 162 us (0.970)
  Pallas kernels: 165 us -> 158 us
    pallas_call x1, Pallas kernels: 165 us -> 158 us  [per_device(): pl.pallas_call(kernel, out_shape=jax.ShapeDtypeStruct((2, *queries.shape)...]
where the time goes in v6:
time: 162 us; the launch traced here: 161 us
  Pallas kernels  158 us (98%)
  local copies, waits for them, and re-layouts  1.75 us (1%)
    pallas_call x1, Pallas kernels, per_device(): pl.pallas_call(kernel, out_shape=jax.ShapeDtypeStruct((2, *queries.shape)...  158 us

profile of v6, /device:TPU:1, one launch (start us, length us, event | category | flops | bytes accessed | tf_op | source)
XLA Modules:
  0.0 160.8 jit_solution(17429144375390152747)
XLA Ops:
  0.6 158.4 %layer.1 = bf16[2,128,640]{2,1,0:T(8,128)(2,1)} custom-call(bf16[128,640]{1,0:T(8,128)(2,1)} %q_hbm.1, bf16[128,128]{1,0:T(8,128)(2,1)} %k_hbm.1, bf16[128,128]{1,0:T(8,128)(2,1)} %v_hbm.1, s32[64]{0:T(128)} %order_hbm.1, s32[1,128]{1,0:T(1,128)} %bitcast.15, f32[1,5120]{1,0:T(1,128)} %bitcast.14, f32[8,5120]{1,0:T(8,128)} %bitcast.13, ...), custom_call_target="tpu_custom_call" | custom-call | tf_op jit(solution)/shard_map/layer/pallas_call | solution.py:607
  159.0 1.7 %slice_bitcast_fusion = (bf16[128,640]{1,0:T(8,128)(2,1)}, bf16[128,640]{1,0:T(8,128)(2,1)}) fusion(bf16[2,128,640]{2,1,0:T(8,128)(2,1)} %layer.1), kind=kLoop, calls=%fused_computation | loop fusion | bytes 655360 | tf_op jit(solution)/shard_map/squeeze | solution.py:669

commit v7 on v6

--- a/solution.py
+++ b/solution.py
@@ -31,16 +31,19 @@
 OFFS = (0, -1, 1, 2)
 OPPOSITE = ((0, 0), (1, 1), (2, 1), (3, 0))
 
+HANDED = (0, 1)
+
 
 class Gather:
-    def __init__(self, tori, piece, half, rows, ssem, rsem, send, arrived):
+    def __init__(self, whole, tori, piece, half, rows, ssem, rsem, send, arrived):
+        self.whole = whole
         self.tori, self.piece, self.half, self.rows = tori, piece, half, rows
         self.ssem, self.rsem, self.send, self.arrived = ssem, rsem, send, arrived
 
     def second(self, t, i):
         piece = self.piece(t, OFFS[i], 0)
         for s, dq in ((0, 1), (1, -1)):
-            r = 4 + i if s == OPPOSITE[i][1] else 8
+            r = 4 + i if s == OPPOSITE[i][1] and (self.whole or i not in HANDED) else 8
             self.send(piece, piece, self.ssem.at[2], self.rsem.at[r], t.dev(0, dq))
 
     def start(self, t):
@@ -66,13 +69,18 @@
 
     def forward(self, i):
         dq = 1 if OPPOSITE[i][1] == 0 else -1
+        if i in HANDED and not self.whole:
+            return
         self.arrived(self.rows(2), self.rsem.at[4 + i])
         for t in self.tori:
             piece = self.piece(t, OFFS[i], -dq)
-            self.send(piece, piece, self.ssem.at[3], self.rsem.at[8], t.dev(0, dq))
+            self.send(piece, piece, self.ssem.at[3], self.rsem.at[9 if i in HANDED else 8], t.dev(0, dq))
+
+    def handed(self):
+        self.arrived(self.rows(2 * len(HANDED)), self.rsem.at[9])
 
     def done(self):
-        self.arrived(self.rows(16), self.rsem.at[8])
+        self.arrived(self.rows(16 - 2 * len(HANDED) if self.whole else 16), self.rsem.at[8])
 
 
 class Torus:
@@ -378,6 +386,7 @@
 
     gather = [
         Gather(
+            w == 0,
             tori,
             lambda t, dp, dq, w=w: g.at[w, t.h, t.rows(dp, dq)],
             lambda t, dp, dq, s, w=w: g.at[w, t.h, t.rows(dp, dq), pl.ds(s * PIECE_COLS, PIECE_COLS)],
@@ -389,6 +398,13 @@
         )
         for w in range(PLANES)
     ]
+
+    def hand_over():
+        gather[0].handed()
+        for i in HANDED:
+            for t in tori:
+                rows = t.rows(OFFS[i], 2)
+                send(g.at[0, t.h, rows], g.at[1, t.h, rows], ag_s.at[4], ag_r.at[1, 9], column(other, 0))
 
     def ffn(w, h):
         step = 1280
@@ -526,6 +542,7 @@
         gather[1].start(t)
     gather[0].forward(2)
     gather[0].forward(3)
+    hand_over()
     gather[1].near()
     gather[1].far()
     loads[0].wait()
@@ -541,6 +558,7 @@
     rs_begin(a)
     rs_begin(p)
     gather[1].done()
+    gather[1].handed()
     rs_join(a)
     ffn(1, 0)
     ffn(1, 1)
@@ -591,7 +609,8 @@
     all_sent(g.at[0, 0, pl.ds(0, 8 * HALF)], ag_s.at[0])
     all_sent(g.at[0, 0, pl.ds(0, 4 * HALF)], ag_s.at[1])
     all_sent(g.at[0], ag_s.at[2])
-    all_sent(g.at[0, 0], ag_s.at[3])
+    all_sent(g.at[0, 0, pl.ds(0, (16 - 2 * len(HANDED)) * HALF)], ag_s.at[3])
+    all_sent(g.at[0, 0, pl.ds(0, 2 * len(HANDED) * HALF)], ag_s.at[4])
     for i, ref in enumerate((ru1, ru2, rv1, rv2)):
         all_sent(ref, rs_s.at[i])
     all_sent(ret.at[0, pl.ds(0, EXPERTS - 1)], back_s.at[0])
@@ -643,8 +662,8 @@
             dma((13,)),
             dma((2,)),
             dma((3,)),
-            dma((4,)),
-            dma((PLANES, 9)),
+            dma((5,)),
+            dma((PLANES, 10)),
             dma((4,)),
             dma((5, 10)),
             dma((2,)),

time: 162 us -> 160 us (0.988)
  no operation moved by 1% of the time
where the time goes in v7:
time: 160 us; the launch traced here: 159 us
  Pallas kernels  157 us (98%)
  local copies, waits for them, and re-layouts  1.75 us (1%)
    pallas_call x1, Pallas kernels, per_device(): pl.pallas_call(kernel, out_shape=jax.ShapeDtypeStruct((2, *queries.shape)...  157 us

profile of v7, /device:TPU:1, one launch (start us, length us, event | category | flops | bytes accessed | tf_op | source)
XLA Modules:
  0.0 159.3 jit_solution(7382445128186189697)
XLA Ops:
  0.6 156.9 %layer.1 = bf16[2,128,640]{2,1,0:T(8,128)(2,1)} custom-call(bf16[128,640]{1,0:T(8,128)(2,1)} %q_hbm.1, bf16[128,128]{1,0:T(8,128)(2,1)} %k_hbm.1, bf16[128,128]{1,0:T(8,128)(2,1)} %v_hbm.1, s32[64]{0:T(128)} %order_hbm.1, s32[1,128]{1,0:T(1,128)} %bitcast.15, f32[1,5120]{1,0:T(1,128)} %bitcast.14, f32[8,5120]{1,0:T(8,128)} %bitcast.13, ...), custom_call_target="tpu_custom_call" | custom-call | tf_op jit(solution)/shard_map/layer/pallas_call | solution.py:626
  157.6 1.7 %slice_bitcast_fusion = (bf16[128,640]{1,0:T(8,128)(2,1)}, bf16[128,640]{1,0:T(8,128)(2,1)}) fusion(bf16[2,128,640]{2,1,0:T(8,128)(2,1)} %layer.1), kind=kLoop, calls=%fused_computation | loop fusion | bytes 655360 | tf_op jit(solution)/shard_map/squeeze | solution.py:688

commit v8 on v7

--- a/solution.py
+++ b/solution.py
@@ -585,8 +585,22 @@
     rs_last(q)
     rs_finish(q)
 
+    all_sent(kv.at[0, 0, 0, pl.ds(0, 2)], kv_s.at[0])
+    all_sent(kv.at[0, 0, pl.ds(0, SIDE - 1)], kv_s.at[1])
+    all_sent(kv.at[:, :, pl.ds(0, 2)], kv_s.at[2])
+    all_sent(kv.at[:, :, 0], kv_s.at[3])
+    all_sent(xin.at[0, pl.ds(0, EXPERTS - 1)], a2a_s.at[0])
+    all_sent(xin.at[1], a2a_s.at[1])
+    all_sent(g.at[0, 0, pl.ds(0, 8 * HALF)], ag_s.at[0])
+    all_sent(g.at[0, 0, pl.ds(0, 4 * HALF)], ag_s.at[1])
+    all_sent(g.at[0], ag_s.at[2])
+    all_sent(g.at[0, 0, pl.ds(0, (16 - 2 * len(HANDED)) * HALF)], ag_s.at[3])
+    all_sent(g.at[0, 0, pl.ds(0, 2 * len(HANDED) * HALF)], ag_s.at[4])
+    for i, ref in enumerate((ru1, ru2, rv1, rv2)):
+        all_sent(ref, rs_s.at[i])
+
     routed = None
-    for w in range(PLANES):
+    for w in (1, 0):
         arrived(ret.at[w, pl.ds(0, EXPERTS - 1 + w)], back_r.at[w])
         if w == 0:
             mine.wait()
@@ -600,19 +614,6 @@
     result.start()
     attended.wait()
     result.wait()
-    all_sent(kv.at[0, 0, 0, pl.ds(0, 2)], kv_s.at[0])
-    all_sent(kv.at[0, 0, pl.ds(0, SIDE - 1)], kv_s.at[1])
-    all_sent(kv.at[:, :, pl.ds(0, 2)], kv_s.at[2])
-    all_sent(kv.at[:, :, 0], kv_s.at[3])
-    all_sent(xin.at[0, pl.ds(0, EXPERTS - 1)], a2a_s.at[0])
-    all_sent(xin.at[1], a2a_s.at[1])
-    all_sent(g.at[0, 0, pl.ds(0, 8 * HALF)], ag_s.at[0])
-    all_sent(g.at[0, 0, pl.ds(0, 4 * HALF)], ag_s.at[1])
-    all_sent(g.at[0], ag_s.at[2])
-    all_sent(g.at[0, 0, pl.ds(0, (16 - 2 * len(HANDED)) * HALF)], ag_s.at[3])
-    all_sent(g.at[0, 0, pl.ds(0, 2 * len(HANDED) * HALF)], ag_s.at[4])
-    for i, ref in enumerate((ru1, ru2, rv1, rv2)):
-        all_sent(ref, rs_s.at[i])
     all_sent(ret.at[0, pl.ds(0, EXPERTS - 1)], back_s.at[0])
     all_sent(ret.at[1], back_s.at[1])
 

time: 160 us -> 160 us (level)
  no operation moved by 1% of the time
where the time goes in v8:
time: 160 us; the launch traced here: 159 us
  Pallas kernels  157 us (98%)
  local copies, waits for them, and re-layouts  1.75 us (1%)
    pallas_call x1, Pallas kernels, per_device(): pl.pallas_call(kernel, out_shape=jax.ShapeDtypeStruct((2, *queries.shape)...  157 us

profile of v8, /device:TPU:1, one launch (start us, length us, event | category | flops | bytes accessed | tf_op | source)
XLA Modules:
  0.0 159.3 jit_solution(3150987049211562666)
XLA Ops:
  0.6 156.9 %layer.1 = bf16[2,128,640]{2,1,0:T(8,128)(2,1)} custom-call(bf16[128,640]{1,0:T(8,128)(2,1)} %q_hbm.1, bf16[128,128]{1,0:T(8,128)(2,1)} %k_hbm.1, bf16[128,128]{1,0:T(8,128)(2,1)} %v_hbm.1, s32[64]{0:T(128)} %order_hbm.1, s32[1,128]{1,0:T(1,128)} %bitcast.15, f32[1,5120]{1,0:T(1,128)} %bitcast.14, f32[8,5120]{1,0:T(8,128)} %bitcast.13, ...), custom_call_target="tpu_custom_call" | custom-call | tf_op jit(solution)/shard_map/layer/pallas_call | solution.py:627
  157.5 1.7 %slice_bitcast_fusion = (bf16[128,640]{1,0:T(8,128)(2,1)}, bf16[128,640]{1,0:T(8,128)(2,1)}) fusion(bf16[2,128,640]{2,1,0:T(8,128)(2,1)} %layer.1), kind=kLoop, calls=%fused_computation | loop fusion | bytes 655360 | tf_op jit(solution)/shard_map/squeeze | solution.py:689
